TPU v7x, 32 devices: a whole 2x2x4 slice. The times are simulated.
32 devices in a mesh: blk: 16 (over z, x, core), rep: 2 (over y).
Axes of the slice: x: 2, y: 2, z: 4, core: 2. Of those that a mesh axis runs over, the one named last changes fastest.
Arguments:
- tokens: int32 [8192, 69], P('blk'), may hold values from 0 to 63
- lengths: int32 [8192], P('blk'), may hold values from 16 to 69
- embed: bfloat16 [64, 256], replicated, may hold values from -6 to 6
- conv_w: bfloat16 [7, 32, 256], replicated, may hold values from -0.375 to 0.375
- conv_b: float32 [256], replicated, may hold values from -3 to 3
- inv_len: float32 [256], replicated, may hold values from 0.05 to 0.3
- hyper: float32 [2], replicated, may hold values from 0.5 to 2
- probes: bfloat16 [8192, 64], P('blk'), may hold values from -6 to 6
- prev_probes: bfloat16 [8192, 64], P(('blk', 'rep')), may hold values from -6 to 6
- coupling: float32 [64, 64], replicated, may hold values from -12 to 12
Outputs:
- block_a: float32 [64, 64], replicated
- block_r: float32 [64, 64], replicated
- next_probes: float32 [8192, 64], P(('blk', 'rep'))
All inputs are finite; a program needn't handle non-finite values.
Results may differ from a plain program's by a relative error of at most 0.0065.
Values may be sent and summed in bfloat16 or wider, within the bound.
A program may use at most 128 MiB of HBM per device.

v0:
```python
import math

import jax
import jax.numpy as jnp
from jax import lax
from jax.sharding import PartitionSpec as P


def upper_factor(gram):
    order = gram.shape[0]
    index_row = jnp.arange(order, dtype=jnp.int32)

    def column_step(column, carry):
        work, lower = carry
        pivot = lax.dynamic_slice(work, (column, column), (1, 1))[0, 0]
        vector = lax.dynamic_slice_in_dim(work, column, 1, 1)[:, 0]
        vector = jnp.where(index_row >= column, vector * lax.rsqrt(pivot), 0.0)
        lower = lower + vector[:, None] * (index_row == column).astype(jnp.float32)[None, :]
        work = work - vector[:, None] * vector[None, :]
        return (work, lower)

    _, lower = lax.fori_loop(0, order, column_step, (gram, jnp.zeros_like(gram)))
    return lower.T


def upper_inverse(upper):
    order = upper.shape[0]
    index_row = jnp.arange(order, dtype=jnp.int32)

    def row_step(count, solved):
        row = order - 1 - count
        upper_row = lax.dynamic_slice_in_dim(upper, row, 1, 0)
        diag_value = lax.dynamic_slice(upper, (row, row), (1, 1))[0, 0]
        unit_row = (index_row == row).astype(jnp.float32)[None, :]
        product = jnp.dot(
            upper_row, solved, precision=lax.Precision.HIGHEST, preferred_element_type=jnp.float32
        )
        new_row = (unit_row - product) / diag_value
        return solved + (index_row == row).astype(jnp.float32)[:, None] * new_row

    return lax.fori_loop(0, order, row_step, jnp.zeros_like(upper))


def dense_taps(conv_w, channels):
    tap_count, group_width, _ = conv_w.shape
    group_count = channels // group_width
    tiled = jnp.tile(conv_w, (1, group_count, 1))
    in_group = jnp.arange(channels, dtype=jnp.int32) // group_width
    same_group = (in_group[:, None] == in_group[None, :]).astype(jnp.bfloat16)
    return tiled * same_group[None, :, :]


def conv_features(tokens, lengths, embed, conv_w, conv_b, inv_len):
    row_count, seq_len = tokens.shape
    vocab_size, channels = embed.shape
    tap_count = conv_w.shape[0]
    positions = (seq_len - tap_count) // 2 + 1
    block_rows = math.gcd(row_count, 256)
    block_count = row_count // block_rows
    tap_weights = dense_taps(conv_w, channels)
    vocab_ids = jnp.arange(vocab_size, dtype=jnp.int32)[None, :]

    def one_block(pair):
        tok_block, len_block = pair
        running = jnp.zeros((block_rows * positions, channels), jnp.float32)
        for tap_index in range(tap_count):
            tap_tokens = lax.slice(
                tok_block, (0, tap_index), (block_rows, tap_index + 2 * (positions - 1) + 1), (1, 2)
            )
            onehot = (tap_tokens.reshape(-1, 1) == vocab_ids).astype(jnp.bfloat16)
            embedded = jnp.dot(onehot, embed, preferred_element_type=jnp.float32).astype(
                jnp.bfloat16
            )
            running = running + jnp.dot(
                embedded, tap_weights[tap_index], preferred_element_type=jnp.float32
            )
        preact = running.reshape(block_rows, positions, channels) + conv_b
        counts = (len_block - tap_count) // 2 + 1
        valid_mask = (jnp.arange(positions, dtype=jnp.int32)[None, :] < counts[:, None]).astype(
            jnp.float32
        )
        activated = jax.nn.gelu(preact, approximate=True) * valid_mask[:, :, None]
        pooled = jnp.sum(activated, axis=1) / counts.astype(jnp.float32)[:, None]
        row_mean = jnp.mean(pooled, axis=1, keepdims=True)
        centered = pooled - row_mean
        row_var = jnp.mean(centered * centered, axis=1, keepdims=True)
        normed = centered * lax.rsqrt(row_var + 1e-05)
        return (normed * inv_len).astype(jnp.bfloat16)

    result = lax.map(
        one_block,
        (
            tokens.reshape(block_count, block_rows, seq_len),
            lengths.reshape(block_count, block_rows),
        ),
    )
    return result.reshape(row_count, channels)


def squares_of(feat_rows):
    wide = feat_rows.astype(jnp.float32)
    return jnp.sum(wide * wide, axis=1)


def kernel_block(rows_feat, rows_sq, amplitude, col_feat, col_probes):
    col_sq = squares_of(col_feat)
    inner_prod = lax.dot_general(
        rows_feat, col_feat, (((1,), (1,)), ((), ())), preferred_element_type=jnp.float32
    )
    distance = jnp.maximum(rows_sq[:, None] + col_sq[None, :] - 2.0 * inner_prod, 0.0)
    weights = (amplitude * jnp.exp(-0.5 * distance)).astype(jnp.bfloat16)
    return jnp.dot(weights, col_probes, preferred_element_type=jnp.float32)


def make_fold(rows_feat, amplitude):
    rows_sq = squares_of(rows_feat)

    def accumulate(running, piece, first_row):
        col_feat, col_probes = piece
        col_count = col_feat.shape[0]
        col_width = math.gcd(col_count, 1024)
        col_blocks = col_feat.reshape(col_count // col_width, col_width, col_feat.shape[1])
        probe_blocks = col_probes.reshape(col_count // col_width, col_width, col_probes.shape[1])

        def advance(partial_value, block_pair):
            return (
                partial_value
                + kernel_block(rows_feat, rows_sq, amplitude, block_pair[0], block_pair[1]),
                None,
            )

        result, _ = lax.scan(advance, running, (col_blocks, probe_blocks))
        return result

    return accumulate


def gram_of(left, right):
    return lax.dot_general(
        left,
        right,
        (((0,), (0,)), ((), ())),
        precision=lax.Precision.HIGHEST,
        preferred_element_type=jnp.float32,
    )


def per_device(
    tokens, lengths, embed, conv_w, conv_b, inv_len, hyper, probes, prev_probes, coupling
):
    feat = conv_features(tokens, lengths, embed, conv_w, conv_b, inv_len)
    row_count = feat.shape[0]
    probe_width = probes.shape[1]
    half_rows = row_count // lax.axis_size("rep")
    rep_index = lax.axis_index("rep")
    total_rows = row_count * lax.axis_size("blk")
    inv_root = 1.0 / math.sqrt(total_rows)
    amplitude = hyper[0]
    noise_var = hyper[1]
    own_feat = lax.dynamic_slice_in_dim(feat, rep_index * half_rows, half_rows, 0)
    own_probes = lax.dynamic_slice_in_dim(probes, rep_index * half_rows, half_rows, 0)
    accumulate = make_fold(own_feat, amplitude)
    initial = jnp.zeros((half_rows, probe_width), jnp.float32)
    applied = accumulate(
        initial,
        (
            lax.all_gather(feat, "blk", axis=0, tiled=True),
            lax.all_gather(probes, "blk", axis=0, tiled=True),
        ),
        jnp.int32(0),
    )
    own_wide = own_probes.astype(jnp.float32)
    applied = applied + noise_var * own_wide
    basis_half = own_wide * inv_root
    coupled = (
        jnp.dot(
            prev_probes.astype(jnp.float32),
            coupling.T,
            precision=lax.Precision.HIGHEST,
            preferred_element_type=jnp.float32,
        )
        * inv_root
    )
    image = applied * inv_root - coupled
    block_a, cross_gram, correlation = lax.psum(
        (gram_of(basis_half, image), gram_of(image, image), gram_of(basis_half, basis_half)),
        ("blk", "rep"),
    )
    resid = image - jnp.dot(
        basis_half, block_a, precision=lax.Precision.HIGHEST, preferred_element_type=jnp.float32
    )
    squared_a = gram_of(block_a, block_a)
    middle = jnp.dot(
        correlation, block_a, precision=lax.Precision.HIGHEST, preferred_element_type=jnp.float32
    )
    gram = cross_gram - 2.0 * squared_a + gram_of(block_a, middle)
    upper = upper_factor(gram)
    inverse = upper_inverse(upper)
    next_probes = jnp.dot(
        resid, inverse, precision=lax.Precision.HIGHEST, preferred_element_type=jnp.float32
    ) * math.sqrt(total_rows)
    return (block_a, upper, next_probes)


def solution(mesh):
    return jax.shard_map(
        per_device,
        mesh=mesh,
        in_specs=(
            P("blk", None),
            P("blk"),
            P(),
            P(),
            P(),
            P(),
            P(),
            P("blk", None),
            P(("blk", "rep"), None),
            P(),
        ),
        out_specs=(P(), P(), P(("blk", "rep"), None)),
        check_vma=False,
    )
```

profile of v0, /device:TPU:0, one launch (start us, length us, event | category | flops | bytes accessed | tf_op | source)
XLA Modules:
  0.0 449.3 jit_solution(9083726224631468537)
XLA Ops:
  10.8 118.5 %while.58 = (s32[]{:T(128)}, bf16[2,256,256]{2,1,0:T(8,128)(2,1)S(1)}, s32[2,256,69]{2,1,0:T(8,128)S(1)}, bf16[64,256]{1,0:T(8,128)(2,1)}, bf16[7,256,256]{2,1,0...) while((s32[]{:T(128)}, ...), condition=%wide.region_4.5_spmd.clone.clone, body=%wide.region_0.4_spmd.clone.clone.sunk | while | flops 9449918464 | bytes 104601792 | solution.py:90
  12.2 6.5 %fusion.176 = f32[8192,256]{1,0:T(8,128)} fusion(bf16[64,256]{1,0:T(8,128)(2,1)} %get-tuple-element.699, s32[8192]{0:T(1024)S(1)} %eq.423, bf16[7,256,256]{2,1,0:T(8,128)(2,1)S(1)} %get-tuple-element.700), kind=kOutput, calls=%fused_computation.33.clone.1 | convolution fusion | flops 1344798720 | bytes 8585216 | tf_op jit(solution)/shard_map/while/body/eval_jaxpr/dot_general | solution.py:74
  18.7 1.3 slice.174
  20.1 7.0 %convolution_add_fusion.12 = f32[8192,256]{1,0:T(8,128)} fusion(f32[8192,256]{1,0:T(8,128)} %fusion.176, bf16[64,256]{1,0:T(8,128)(2,1)S(1)} %copy-done.1, s32[8192]{0:T(1024)S(1)} %eq.424, bf16[7,256,256]{2,1,0:T(8,128)(2,1)S(1)} %get-tuple-element.700), kind=kOutput, calls=%fused_computation.9.clone.1 | convolution fusion | flops 1346895872 | bytes 16973824 | tf_op jit(solution)/shard_map/while/body/eval_jaxpr/dot_general | solution.py:74
  27.1 1.3 slice.175
  28.5 7.0 %convolution_add_fusion.13 = f32[8192,256]{1,0:T(8,128)} fusion(f32[8192,256]{1,0:T(8,128)} %convolution_add_fusion.12, bf16[64,256]{1,0:T(8,128)(2,1)S(1)} %copy-done.1, s32[8192]{0:T(1024)S(1)} %eq.425, bf16[7,256,256]{2,1,0:T(8,128)(2,1)S(1)} %get-tuple-element.700), kind=kOutput, calls=%fused_computation.8.clone.1 | convolution fusion | flops 1346895872 | bytes 16973824 | tf_op jit(solution)/shard_map/while/body/eval_jaxpr/dot_general | solution.py:74
  35.5 1.3 slice.176
  36.8 7.0 %convolution_add_fusion.14 = f32[8192,256]{1,0:T(8,128)} fusion(f32[8192,256]{1,0:T(8,128)} %convolution_add_fusion.13, bf16[64,256]{1,0:T(8,128)(2,1)S(1)} %copy-done.1, s32[8192]{0:T(1024)S(1)} %eq.426, bf16[7,256,256]{2,1,0:T(8,128)(2,1)S(1)} %get-tuple-element.700), kind=kOutput, calls=%fused_computation.7.clone.1 | convolution fusion | flops 1346895872 | bytes 16973824 | tf_op jit(solution)/shard_map/while/body/eval_jaxpr/dot_general | solution.py:74
  43.8 1.3 slice.177
  45.2 7.0 %convolution_add_fusion.15 = f32[8192,256]{1,0:T(8,128)} fusion(f32[8192,256]{1,0:T(8,128)} %convolution_add_fusion.14, bf16[64,256]{1,0:T(8,128)(2,1)S(1)} %copy-done.1, s32[8192]{0:T(1024)S(1)} %eq.427, bf16[7,256,256]{2,1,0:T(8,128)(2,1)S(1)} %get-tuple-element.700), kind=kOutput, calls=%fused_computation.6.clone.1 | convolution fusion | flops 1346895872 | bytes 16973824 | tf_op jit(solution)/shard_map/while/body/eval_jaxpr/dot_general | solution.py:74
  52.2 1.3 slice.178
  53.6 7.0 %convolution_add_fusion.16 = f32[8192,256]{1,0:T(8,128)} fusion(f32[8192,256]{1,0:T(8,128)} %convolution_add_fusion.15, bf16[64,256]{1,0:T(8,128)(2,1)S(1)} %copy-done.1, s32[8192]{0:T(1024)S(1)} %eq.428, bf16[7,256,256]{2,1,0:T(8,128)(2,1)S(1)} %get-tuple-element.700), kind=kOutput, calls=%fused_computation.5.clone.1 | convolution fusion | flops 1346895872 | bytes 16973824 | tf_op jit(solution)/shard_map/while/body/eval_jaxpr/dot_general | solution.py:74
  60.6 1.3 slice.179
  62.1 7.3 %fusion.177 = f32[256,256]{1,0:T(8,128)S(1)} fusion(f32[256,32]{1,0:T(8,128)S(1)} %fusion.175, f32[256]{0:T(256)S(1)} %copy-done.7, f32[8192,256]{1,0:T(8,128)} %convolution_add_fusion.16, bf16[7,256,256]{2,1,0:T(8,128)(2,1)S(1)} %get-tuple-element.700, bf16[64,256]{1,0:T(8,128)(2,1)S(1)} %copy-done.1, s32[8192]{0:T(1024)S(1)} %eq.429), kind=kOutput, calls=%fused_computation.32.clone.1 | convolution fusion | flops 1369899008 | bytes 8979456 | tf_op jit(solution)/shard_map/while/body/eval_jaxpr/dot_general | solution.py:74
  71.4 6.5 %fusion.176 = f32[8192,256]{1,0:T(8,128)} fusion(bf16[64,256]{1,0:T(8,128)(2,1)} %get-tuple-element.699, s32[8192]{0:T(1024)S(1)} %eq.423, bf16[7,256,256]{2,1,0:T(8,128)(2,1)S(1)} %get-tuple-element.700), kind=kOutput, calls=%fused_computation.33.clone.1 | convolution fusion | flops 1344798720 | bytes 8585216 | tf_op jit(solution)/shard_map/while/body/eval_jaxpr/dot_general | solution.py:74
  77.9 1.3 slice.174
  79.3 7.0 %convolution_add_fusion.12 = f32[8192,256]{1,0:T(8,128)} fusion(f32[8192,256]{1,0:T(8,128)} %fusion.176, bf16[64,256]{1,0:T(8,128)(2,1)S(1)} %copy-done.1, s32[8192]{0:T(1024)S(1)} %eq.424, bf16[7,256,256]{2,1,0:T(8,128)(2,1)S(1)} %get-tuple-element.700), kind=kOutput, calls=%fused_computation.9.clone.1 | convolution fusion | flops 1346895872 | bytes 16973824 | tf_op jit(solution)/shard_map/while/body/eval_jaxpr/dot_general | solution.py:74
  86.3 1.3 slice.175
  87.6 7.0 %convolution_add_fusion.13 = f32[8192,256]{1,0:T(8,128)} fusion(f32[8192,256]{1,0:T(8,128)} %convolution_add_fusion.12, bf16[64,256]{1,0:T(8,128)(2,1)S(1)} %copy-done.1, s32[8192]{0:T(1024)S(1)} %eq.425, bf16[7,256,256]{2,1,0:T(8,128)(2,1)S(1)} %get-tuple-element.700), kind=kOutput, calls=%fused_computation.8.clone.1 | convolution fusion | flops 1346895872 | bytes 16973824 | tf_op jit(solution)/shard_map/while/body/eval_jaxpr/dot_general | solution.py:74
  94.6 1.3 slice.176
  96.0 7.0 %convolution_add_fusion.14 = f32[8192,256]{1,0:T(8,128)} fusion(f32[8192,256]{1,0:T(8,128)} %convolution_add_fusion.13, bf16[64,256]{1,0:T(8,128)(2,1)S(1)} %copy-done.1, s32[8192]{0:T(1024)S(1)} %eq.426, bf16[7,256,256]{2,1,0:T(8,128)(2,1)S(1)} %get-tuple-element.700), kind=kOutput, calls=%fused_computation.7.clone.1 | convolution fusion | flops 1346895872 | bytes 16973824 | tf_op jit(solution)/shard_map/while/body/eval_jaxpr/dot_general | solution.py:74
  103.0 1.3 slice.177
  104.4 7.0 %convolution_add_fusion.15 = f32[8192,256]{1,0:T(8,128)} fusion(f32[8192,256]{1,0:T(8,128)} %convolution_add_fusion.14, bf16[64,256]{1,0:T(8,128)(2,1)S(1)} %copy-done.1, s32[8192]{0:T(1024)S(1)} %eq.427, bf16[7,256,256]{2,1,0:T(8,128)(2,1)S(1)} %get-tuple-element.700), kind=kOutput, calls=%fused_computation.6.clone.1 | convolution fusion | flops 1346895872 | bytes 16973824 | tf_op jit(solution)/shard_map/while/body/eval_jaxpr/dot_general | solution.py:74
  111.4 1.3 slice.178
  112.7 7.0 %convolution_add_fusion.16 = f32[8192,256]{1,0:T(8,128)} fusion(f32[8192,256]{1,0:T(8,128)} %convolution_add_fusion.15, bf16[64,256]{1,0:T(8,128)(2,1)S(1)} %copy-done.1, s32[8192]{0:T(1024)S(1)} %eq.428, bf16[7,256,256]{2,1,0:T(8,128)(2,1)S(1)} %get-tuple-element.700), kind=kOutput, calls=%fused_computation.5.clone.1 | convolution fusion | flops 1346895872 | bytes 16973824 | tf_op jit(solution)/shard_map/while/body/eval_jaxpr/dot_general | solution.py:74
  119.7 1.3 slice.179
  121.3 7.3 %fusion.177 = f32[256,256]{1,0:T(8,128)S(1)} fusion(f32[256,32]{1,0:T(8,128)S(1)} %fusion.175, f32[256]{0:T(256)S(1)} %copy-done.7, f32[8192,256]{1,0:T(8,128)} %convolution_add_fusion.16, bf16[7,256,256]{2,1,0:T(8,128)(2,1)S(1)} %get-tuple-element.700, bf16[64,256]{1,0:T(8,128)(2,1)S(1)} %copy-done.1, s32[8192]{0:T(1024)S(1)} %eq.429), kind=kOutput, calls=%fused_computation.32.clone.1 | convolution fusion | flops 1369899008 | bytes 8979456 | tf_op jit(solution)/shard_map/while/body/eval_jaxpr/dot_general | solution.py:74
  132.0 2.0 copy.20
  134.0 49.5 %all-gather.3.cloned.1.call-done = bf16[8192,256]{1,0:T(8,128)(2,1)} async-done(((bf16[512,256]{1,0:T(8,128)(2,1)}), bf16[8192,256]{1,0:T(8,128)(2,1)}) %all-gather.3.cloned.1.call-update) | async-done | bytes 4194320 | tf_op jit(solution)/shard_map/all_gather | solution.py:167
  183.5 29.2 %while.59 = (s32[]{:T(128)}, f32[256,64]{0,1:T(8,128)S(1)}, f32[]{:T(128)}, f32[256]{0:T(256)S(1)}, bf16[8,1024,256]{2,1,0:T(8,128)(2,1)}, /*index=5*/bf16[256,2...) while((s32[]{:T(128)}, f32[256,64]{0,1:T(8,128)S(1)}, f32[]{:T(128)}, ...), condition=%wide.region_8.9_spmd.clone, body=%wide.region_6.8_spmd.clone.sunk | while | flops 170425344 | bytes 1583723 | solution.py:132
  183.5 1.3 multiply_reduce_fusion.6
  184.8 2.4 fusion.183
  187.2 1.3 multiply_reduce_fusion.6
  188.4 2.4 fusion.183
  190.8 1.3 multiply_reduce_fusion.6
  192.1 2.4 fusion.183
  194.5 1.3 multiply_reduce_fusion.6
  195.7 2.4 fusion.183
  198.1 1.3 multiply_reduce_fusion.6
  199.4 2.4 fusion.183
  201.8 1.3 multiply_reduce_fusion.6
  203.0 2.4 fusion.183
  205.4 1.3 multiply_reduce_fusion.6
  206.7 2.4 fusion.183
  210.3 2.4 fusion.183
  214.0 40.4 %all-reduce = (f32[64,64]{1,0:T(8,128)S(1)}, f32[64,64]{1,0:T(8,128)S(1)}, f32[64,64]{1,0:T(8,128)S(1)}) all-reduce(f32[64,64]{1,0:T(8,128)S(1)} %fusion.92, f32[64,64]{1,0:T(8,128)S(1)} %fusion.110, f32[64,64]{1,0:T(8,128)S(1)} %fusion.91), channel_id=1, replica_groups=mesh['blk'=16,'rep'=2] {'blk','rep'}, use_global_device_ids=true, to_apply=%region_9.10 | all-reduce | flops 12288 | bytes 98304 | tf_op jit(solution)/shard_map/psum | solution.py:185
  255.4 92.5 %while.61 = (s32[]{:T(128)}, f32[64,64]{0,1:T(8,128)S(1)}, f32[64,64]{0,1:T(8,128)S(1)}, s32[]{:T(128)}, s32[]{:T(128)}) while((s32[]{:T(128)}, f32[64,64]{0,1:T(8,128)S(1)}, f32[64,64]{0,1:T(8,128)S(1)}, s32[]{:T(128)}, s32[]{:T(128)}) %tuple.135), condition=%wide.region_13.14_spmd.clone.clone, body=%wide.region_12.13_spmd.clone.clone.sunk | while | flops 20995 | bytes 70751 | solution.py:22
  347.9 93.7 %while.60 = (s32[]{:T(128)}, f32[64,64]{1,0:T(8,128)S(1)}, f32[64,64]{1,0:T(8,128)S(1)}, s32[]{:T(128)}, s32[]{:T(128)}, /*index=5*/s32[]{:T(128)}, s32[]{:T(128)}) while((s32[]{:T(128)}, f32[64,64]{1,0:T(8,128)S(1)}, f32[64,64]{1,0:T(8,128)S(1)}, s32[]{:T(128)}, s32[]{:T(128)}, /*index=5*/s32[]{:T(128)}, s32[]{:T(128)}) %tuple.148), condition=%wide.region_15.16_spmd.clone, body=%wide.region_14.15_spmd.clone.sunk | while | flops 65927 | bytes 67234 | solution.py:41
  (663 shorter events, 154.3 us)
Async XLA Ops:
  7.2 205.5 %copy-start = (bf16[256,64]{0,1:T(8,128)(2,1)S(1)}, bf16[256,64]{0,1:T(8,128)(2,1)}, u32[]{:S(2)}) copy-start(bf16[256,64]{0,1:T(8,128)(2,1)} %param.26) | copy-start | bytes 98308
  7.2 124.8 %all-gather.5.cloned.1.call-start = ((), (), s32[]{:S(2)}) async-start(), calls=%async_computation.1 | async-start | bytes 1114112 | tf_op jit(solution)/shard_map/all_gather | solution.py:168
  7.9 175.6 %all-gather.3.cloned.1.call-start = ((), (), s32[]{:S(2)}) async-start(), calls=%async_computation | async-start | bytes 4456448 | tf_op jit(solution)/shard_map/all_gather | solution.py:167
  10.8 119.3 %copy-start.9 = (f32[2]{0:T(128)S(1)}, f32[2]{0:T(128)}, u32[]{:S(2)}) copy-start(f32[2]{0:T(128)} %param.24) | copy-start | bytes 28
  10.8 119.9 %copy-start.5 = (bf16[512,64]{0,1:T(8,128)(2,1)S(1)}, bf16[512,64]{0,1:T(8,128)(2,1)}, u32[]{:S(2)}) copy-start(bf16[512,64]{0,1:T(8,128)(2,1)} %param.25) | copy-start | bytes 196612
  10.8 9.2 %copy-start.1 = (bf16[64,256]{1,0:T(8,128)(2,1)S(1)}, bf16[64,256]{1,0:T(8,128)(2,1)}, u32[]{:S(2)}) copy-start(bf16[64,256]{1,0:T(8,128)(2,1)} %get-tuple-element.699) | copy-start | bytes 98308 | tf_op jit(solution)/shard_map/while
  53.6 8.5 %copy-start.7 = (f32[256]{0:T(256)S(1)}, f32[256]{0:T(256)}, u32[]{:S(2)}) copy-start(f32[256]{0:T(256)} %get-tuple-element.701) | copy-start | bytes 3076 | tf_op jit(solution)/shard_map/while
  60.6 9.2 %copy-start.8 = (f32[256]{0:T(256)S(1)}, f32[256]{0:T(256)}, u32[]{:S(2)}) copy-start(f32[256]{0:T(256)} %get-tuple-element.703) | copy-start | bytes 3076 | tf_op jit(solution)/shard_map/while
  70.0 9.2 %copy-start.1 = (bf16[64,256]{1,0:T(8,128)(2,1)S(1)}, bf16[64,256]{1,0:T(8,128)(2,1)}, u32[]{:S(2)}) copy-start(bf16[64,256]{1,0:T(8,128)(2,1)} %get-tuple-element.699) | copy-start | bytes 98308 | tf_op jit(solution)/shard_map/while
  112.7 8.5 %copy-start.7 = (f32[256]{0:T(256)S(1)}, f32[256]{0:T(256)}, u32[]{:S(2)}) copy-start(f32[256]{0:T(256)} %get-tuple-element.701) | copy-start | bytes 3076 | tf_op jit(solution)/shard_map/while
  119.7 9.2 %copy-start.8 = (f32[256]{0:T(256)S(1)}, f32[256]{0:T(256)}, u32[]{:S(2)}) copy-start(f32[256]{0:T(256)} %get-tuple-element.703) | copy-start | bytes 3076 | tf_op jit(solution)/shard_map/while
  129.3 0.7 copy-start.4
  183.5 29.2 %copy-start.6 = (f32[64,64]{1,0:T(8,128)S(1)}, f32[64,64]{1,0:T(8,128)}, u32[]{:S(2)}) copy-start(f32[64,64]{1,0:T(8,128)} %param.27) | copy-start | bytes 49156
  254.3 188.1 %copy-start.3 = (f32[64,64]{1,0:T(8,128)}, f32[64,64]{1,0:T(8,128)S(1)}, u32[]{:S(2)}) copy-start(f32[64,64]{1,0:T(8,128)S(1)} %get-tuple-element.529) | copy-start | bytes 49156
  441.5 0.9 copy-start.2
Sparse Core Ops, SparseCore 0:
  10.2 39.5 all-gather.4
  130.2 53.2 all-gather.2
where the time goes:
time: 452 us; the launch traced here: 449 us
  matrix products  170 us (38%)
  local copies, waits for them, and re-layouts  99.8 us (22%)
  waiting for transfers between devices  50.2 us (11%)
  loops' own time  48.4 us (11%)
  blocking collectives  40.4 us (9%)
  other arithmetic  26.4 us (6%)
  between operations  14.3 us (3%)
    dot_general x14, matrix products, one_block(): jnp.dot(embedded, tap_weights[tap_index], preferred_element_type=jnp.floa...  97.6 us
    dot_general x64, matrix products, row_step(): jnp.dot(upper_row, solved, precision=lax.Precision.HIGHEST, preferred_ele...  50.1 us
    all_gather x1, waiting for transfers between devices, per_device(): lax.all_gather(feat, 'blk', axis=0, tiled=True)  49.5 us
    another operation x1, loops' own time, upper_factor(): lax.fori_loop(0, order, column_step, (gram, jnp.zeros_like(gram)))  47.4 us
    psum x1, blocking collectives, per_device(): lax.psum((gram_of(basis_half, image), gram_of(image, image), gram_of(basi...  40.4 us
    dynamic_slice x64, local copies, waits for them, and re-layouts, row_step(): diag_value = lax.dynamic_slice(upper, (row, row), (1, 1))[0, 0]  38.1 us
    dynamic_slice x64, local copies, waits for them, and re-layouts, column_step(): pivot = lax.dynamic_slice(work, (column, column), (1, 1))[0, 0]  37.6 us
    dot_general x8, matrix products, kernel_block(): return jnp.dot(weights, col_probes, preferred_element_type=jnp.float32)  18.9 us
  transfers between devices with their start and end apart: 2, of which 1 were waited for; matrix products, arithmetic and copies ran while one was open for 28% of the time, Pallas kernels for 0%

commit v1 on v0

v1 whole, which is shorter than its diff:
```python
import functools
import math

import jax
import jax.numpy as jnp
from jax import lax
from jax.experimental import pallas as pl
from jax.experimental.pallas import tpu as pltpu
from jax.sharding import PartitionSpec as P

F32 = jnp.float32
BF16 = jnp.bfloat16
EXTRA = 16
HIGH = lax.Precision.HIGHEST


def build_table(embed_ref, conv_w_ref, conv_b_ref, table, table_hi, table_lo):
    taps, width, channels = conv_w_ref.shape
    vocab = embed_ref.shape[0]
    groups = channels // width
    in_group = lax.broadcasted_iota(jnp.int32, (channels, channels), 0) // width
    out_group = lax.broadcasted_iota(jnp.int32, (channels, channels), 1) // width
    same = in_group == out_group
    for tap in range(taps):
        tiled = jnp.concatenate([conv_w_ref[tap].astype(F32)] * groups, axis=0)
        dense = jnp.where(same, tiled, 0.0).astype(BF16)
        entry = jnp.dot(embed_ref[...], dense, preferred_element_type=F32)
        if tap == 0:
            entry = entry + conv_b_ref[...]
        table[tap * vocab : (tap + 1) * vocab, :] = entry
    full = table[...].T
    high = full.astype(BF16)
    table_hi[...] = high
    table_lo[...] = (full - high.astype(F32)).astype(BF16)


def pooled_features(
    tokens_ref, lengths_ref, inv_len_ref, first, rows, taps, vocab, padded, onehot, table_hi, table_lo, pooled
):
    seq = tokens_ref.shape[1]
    channels = inv_len_ref.shape[0]
    positions = (seq - taps) // 2 + 1
    padded[...] = jnp.zeros_like(padded)
    padded[:, :seq] = tokens_ref[pl.ds(first, rows), :]
    token_rows = padded[...].T
    vocab_ids = lax.broadcasted_iota(jnp.int32, (vocab, rows), 0)
    for spot in range(seq):
        hit = jnp.broadcast_to(token_rows[spot : spot + 1, :], (vocab, rows)) == vocab_ids
        onehot[spot * vocab : (spot + 1) * vocab, :] = jnp.where(hit, 1.0, 0.0).astype(BF16)
    counts = (lengths_ref[:, pl.ds(first, rows)] - taps) // 2 + 1
    pooled[...] = jnp.zeros_like(pooled)
    root = math.sqrt(2.0 / math.pi)

    def position_step(position, carry):
        start = pl.multiple_of(position * (2 * vocab), 2 * vocab)
        window = onehot[pl.ds(start, taps * vocab), :]
        preact = jnp.dot(table_hi[...], window, preferred_element_type=F32)
        preact = preact + jnp.dot(table_lo[...], window, preferred_element_type=F32)
        inner = preact * (root + (root * 0.044715) * (preact * preact))
        half = jnp.where(position < counts, 0.5, 0.0)
        weighted = preact * half
        pooled[...] += weighted + weighted * jnp.tanh(inner)
        return carry

    lax.fori_loop(0, positions, position_step, 0)
    mean_pool = pooled[...] / counts.astype(F32)
    centered = mean_pool - jnp.mean(mean_pool, axis=0, keepdims=True)
    variance = jnp.mean(centered * centered, axis=0, keepdims=True)
    normed = centered * lax.rsqrt(variance + 1e-05)
    return (normed * inv_len_ref[...]).astype(BF16)


def feature_kernel(
    tokens_ref,
    lengths_ref,
    embed_ref,
    conv_w_ref,
    conv_b_ref,
    inv_len_ref,
    cols_ref,
    rows_ref,
    padded,
    onehot,
    table,
    table_hi,
    table_lo,
    pooled,
):
    rows = cols_ref.shape[1]
    channels = inv_len_ref.shape[0]
    first = pl.multiple_of(lax.axis_index("rep") * rows, rows)
    build_table(embed_ref, conv_w_ref, conv_b_ref, table, table_hi, table_lo)
    feat = pooled_features(
        tokens_ref,
        lengths_ref,
        inv_len_ref,
        first,
        rows,
        conv_w_ref.shape[0],
        embed_ref.shape[0],
        padded,
        onehot,
        table_hi,
        table_lo,
        pooled,
    )
    wide = feat.astype(F32)
    half_sq = -0.5 * jnp.sum(wide * wide, axis=0, keepdims=True)
    cols_ref[:channels, :] = feat
    high = half_sq.astype(BF16).astype(F32)
    middle = (half_sq - high).astype(BF16).astype(F32)
    low = half_sq - high - middle
    order = lax.broadcasted_iota(jnp.int32, (EXTRA, rows), 0)
    tail = jnp.where(order == 0, high, jnp.where(order == 1, middle, jnp.where(order == 2, low, 0.0)))
    cols_ref[channels:, :] = tail.astype(BF16)
    rows_ref[...] = wide.T.astype(BF16)


def apply_kernel(hyper_ref, rows_ref, cols_ref, probes_ref, own_ref, prev_ref, coupling_ref, x_ref, gram_ref, total):
    rows, channels = rows_ref.shape
    blocks = cols_ref.shape[0]
    all_rows = blocks * rows
    width = prev_ref.shape[1]
    wide = rows_ref[...].astype(F32)
    row_half = -0.5 * jnp.sum(wide * wide, axis=1, keepdims=True)
    amplitude = hyper_ref[0]
    total[...] = jnp.zeros_like(total)

    def block_step(block, carry):
        cols = cols_ref[block, :channels, :]
        tail = cols_ref[block, channels:, :].astype(F32)
        col_half = jnp.sum(tail, axis=0, keepdims=True)
        inner = jnp.dot(rows_ref[...], cols, preferred_element_type=F32)
        exponent = jnp.minimum(inner + (row_half + col_half), 0.0)
        weights = (amplitude * jnp.exp(exponent)).astype(BF16)
        start = pl.multiple_of(block * rows, rows)
        total[...] += jnp.dot(weights, probes_ref[pl.ds(start, rows), :], preferred_element_type=F32)
        return carry

    lax.fori_loop(0, blocks, block_step, 0)
    first = pl.multiple_of(lax.axis_index("rep") * rows, rows)
    own = own_ref[pl.ds(first, rows), :].astype(F32)
    root = 1.0 / math.sqrt(all_rows)
    coupled = lax.dot_general(
        prev_ref[...].astype(F32),
        coupling_ref[...],
        (((1,), (1,)), ((), ())),
        precision=HIGH,
        preferred_element_type=F32,
    )
    x_ref[:, :width] = own * root
    x_ref[:, width:] = (total[...] + hyper_ref[1] * own - coupled) * root
    both = x_ref[...]
    gram_ref[...] = jnp.dot(both.T, both, precision=HIGH, preferred_element_type=F32)


def finish_kernel(root, x_ref, sums_ref, a_ref, r_ref, next_ref):
    width = a_ref.shape[0]
    corr = sums_ref[:width, :width]
    block_a = sums_ref[:width, width:]
    cross = sums_ref[width:, width:]
    a_ref[...] = block_a
    resid = x_ref[:, width:] - jnp.dot(x_ref[:, :width], block_a, precision=HIGH, preferred_element_type=F32)
    middle = jnp.dot(corr, block_a, precision=HIGH, preferred_element_type=F32) - 2.0 * block_a
    gram = cross + jnp.dot(block_a.T, middle, precision=HIGH, preferred_element_type=F32)
    row = lax.broadcasted_iota(jnp.int32, (width, width), 0)
    col = lax.broadcasted_iota(jnp.int32, (width, width), 1)
    eye = jnp.where(row == col, 1.0, 0.0)
    work = jnp.concatenate([gram, eye], axis=1)
    done = []
    for step in range(width):
        line = work[step : step + 1, :]
        scale = lax.rsqrt(work[step : step + 1, step : step + 1])
        line = line * scale
        done.append(line)
        if step + 1 < width:
            work = work - (work[:, step : step + 1] * scale) * line
    factor = jnp.concatenate(done, axis=0)
    r_ref[...] = jnp.where(row <= col, factor[:, :width], 0.0)
    inverse = factor[:, width:].T
    next_ref[...] = jnp.dot(resid, inverse, precision=HIGH, preferred_element_type=F32) * root


VMEM = pl.BlockSpec(memory_space=pltpu.VMEM)
SMEM = pl.BlockSpec(memory_space=pltpu.SMEM)
PARAMS = pltpu.CompilerParams(vmem_limit_bytes=48 * 1024 * 1024)


def per_device(tokens, lengths, embed, conv_w, conv_b, inv_len, hyper, probes, prev_probes, coupling):
    rows, width = prev_probes.shape
    vocab, channels = embed.shape
    taps = conv_w.shape[0]
    seq = tokens.shape[1]
    depth = taps * vocab
    cols, own_rows = pl.pallas_call(
        feature_kernel,
        out_shape=(
            jax.ShapeDtypeStruct((channels + EXTRA, rows), BF16),
            jax.ShapeDtypeStruct((rows, channels), BF16),
        ),
        in_specs=[VMEM] * 6,
        out_specs=(VMEM, VMEM),
        scratch_shapes=[
            pltpu.VMEM((rows, 128), jnp.int32),
            pltpu.VMEM((seq * vocab, rows), BF16),
            pltpu.VMEM((depth, channels), F32),
            pltpu.VMEM((channels, depth), BF16),
            pltpu.VMEM((channels, depth), BF16),
            pltpu.VMEM((channels, rows), F32),
        ],
        compiler_params=PARAMS,
    )(tokens, lengths.reshape(1, -1), embed, conv_w, conv_b.reshape(1, -1), inv_len.reshape(-1, 1))
    all_cols = lax.all_gather(cols, ("blk", "rep"), axis=0)
    all_probes = lax.all_gather(probes, "blk", axis=0, tiled=True)
    pair, gram = pl.pallas_call(
        apply_kernel,
        out_shape=(
            jax.ShapeDtypeStruct((rows, 2 * width), F32),
            jax.ShapeDtypeStruct((2 * width, 2 * width), F32),
        ),
        in_specs=[SMEM] + [VMEM] * 6,
        out_specs=(VMEM, VMEM),
        scratch_shapes=[pltpu.VMEM((rows, width), F32)],
        compiler_params=PARAMS,
    )(hyper, own_rows, all_cols, all_probes, probes, prev_probes, coupling)
    sums = lax.psum(gram, ("blk", "rep"))
    root = math.sqrt(all_probes.shape[0])
    return pl.pallas_call(
        functools.partial(finish_kernel, root),
        out_shape=(
            jax.ShapeDtypeStruct((width, width), F32),
            jax.ShapeDtypeStruct((width, width), F32),
            jax.ShapeDtypeStruct((rows, width), F32),
        ),
        in_specs=[VMEM] * 2,
        out_specs=(VMEM, VMEM, VMEM),
        compiler_params=PARAMS,
    )(pair, sums)


def solution(mesh):
    return jax.shard_map(
        per_device,
        mesh=mesh,
        in_specs=(
            P("blk", None),
            P("blk"),
            P(),
            P(),
            P(),
            P(),
            P(),
            P("blk", None),
            P(("blk", "rep"), None),
            P(),
        ),
        out_specs=(P(), P(), P(("blk", "rep"), None)),
        check_vma=False,
    )
```

time: 452 us -> 270 us (0.60)
  matrix products: 170 us -> 0 us
  waiting for transfers between devices: 50.2 us -> 208 us
  local copies, waits for them, and re-layouts: 99.8 us -> 12.8 us
  loops' own time: 48.4 us -> 0 us
  blocking collectives: 40.4 us -> 0 us
  Pallas kernels: 0 us -> 34 us
  other arithmetic: 26.4 us -> 0 us
    dot_general x95 -> x0, matrix products: 170 us -> none  [the longest x14 97.6 us: one_block(): jnp.dot(embedded, tap_weights[tap_index], preferred_element_type=jnp.floa...]
    psum x0 -> x1, waiting for transfers between devices: none -> 116 us  [per_device(): sums = lax.psum(gram, ('blk', 'rep'))]
    dynamic_slice x128 -> x0, local copies, waits for them, and re-layouts: 75.7 us -> none  [the longest x64 38.1 us: row_step(): diag_value = lax.dynamic_slice(upper, (row, row), (1, 1))[0, 0]]
    another operation x4 -> x0, loops' own time: 48.4 us -> none  [the longest x1 47.4 us: upper_factor(): lax.fori_loop(0, order, column_step, (gram, jnp.zeros_like(gram)))]
    all_gather x2, waiting for transfers between devices: 49.5 us -> 91.6 us  [the longest x1 64.7 us: per_device(): all_cols = lax.all_gather(cols, ('blk', 'rep'), axis=0)]
    psum x1 -> x0, blocking collectives: 40.4 us -> none  [per_device(): lax.psum((gram_of(basis_half, image), gram_of(image, image), gram_of(basi...]
    pallas_call x0 -> x3, Pallas kernels: none -> 34 us  [the longest x1 14.9 us: per_device(): pl.pallas_call(apply_kernel, out_shape=(jax.ShapeDtypeStruct((rows, 2 * w...]
    slice x15 -> x0, local copies, waits for them, and re-layouts: 18.2 us -> none  [the longest x14 17.6 us: one_block(): lax.slice(tok_block, (0, tap_index), (block_rows, tap_index + 2 * (positi...]
  transfers between devices with their start and end apart: 2 -> 3, of which waited for: 1 -> 3; matrix products, arithmetic and copies ran while one was open for 28% -> 1% of each run, Pallas kernels for 0% -> 5%
where the time goes in v1:
time: 270 us; the launch traced here: 268 us
  waiting for transfers between devices  208 us (77%)
  Pallas kernels  34 us (13%)
  between operations  13.8 us (5%)
  local copies, waits for them, and re-layouts  12.8 us (5%)
    psum x1, waiting for transfers between devices, per_device(): sums = lax.psum(gram, ('blk', 'rep'))  116 us
    all_gather x1, waiting for transfers between devices, per_device(): all_cols = lax.all_gather(cols, ('blk', 'rep'), axis=0)  64.7 us
    all_gather x1, waiting for transfers between devices, per_device(): all_probes = lax.all_gather(probes, 'blk', axis=0, tiled=True)  26.9 us
    pallas_call x1, Pallas kernels, per_device(): pl.pallas_call(apply_kernel, out_shape=(jax.ShapeDtypeStruct((rows, 2 * w...  14.9 us
    pallas_call x1, Pallas kernels, per_device(): pl.pallas_call(feature_kernel, out_shape=(jax.ShapeDtypeStruct((channels...  12.6 us
    unnamed x21, local copies, waits for them, and re-layouts  11.3 us
    pallas_call x1, Pallas kernels, per_device(): pl.pallas_call(functools.partial(finish_kernel, root), out_shape=(jax.Sha...  6.51 us
  transfers between devices with their start and end apart: 3, of which 3 were waited for; matrix products, arithmetic and copies ran while one was open for 1% of the time, Pallas kernels for 5%

profile of v1, /device:TPU:0, one launch (start us, length us, event | category | flops | bytes accessed | tf_op | source)
XLA Modules:
  0.0 268.3 jit_solution(17410119640830730385)
XLA Ops:
  7.2 0.0 all-gather.4.cloned.1.call-start
  7.2 1.6 copy.20.own_ref
  8.8 0.0 all-gather.4.cloned.1.call-update
  8.8 0.0 all-gather.6.cloned.1.call-start
  8.9 0.8 copy.19.inv_len_ref
  9.7 1.0 copy.18.tokens_ref
  10.8 0.0 copy-start.2
  10.8 0.9 copy-done.2
  11.7 0.0 copy-start.5
  11.7 0.8 copy-done.5
  12.4 0.0 copy-start.6
  12.4 0.7 copy-done.6
  13.1 0.0 copy-start.7
  13.1 0.7 copy-done.7
  13.8 12.6 %shard_map.121 = (bf16[272,256]{1,0:T(8,128)(2,1)}, bf16[256,256]{1,0:T(8,128)(2,1)S(1)}) custom-call(s32[512,69]{1,0:T(8,128)S(1)} %copy.18.tokens_ref, s32[1,512]{1,0:T(1,128)S(1)} %bitcast.4, bf16[64,256]{1,0:T(8,128)(2,1)S(1)} %copy-done.5, bf16[7,32,256]{2,1,0:T(8,128)(2,1)S(1)} %copy-done.2, f32[1,256]{1,0:T(1,128)S(1)} %bitcast.5, ...), custom_call_target="tpu_custom_call" | custom-call | tf_op jit(solution)/shard_map/pallas_call | solution.py:195
  26.4 0.0 all-gather.6.cloned.1.call-update
  26.4 0.0 all-reduce.2.cloned.1.call-start
  26.5 0.9 copy.22.prev_ref
  27.3 26.9 %all-gather.4.cloned.1.call-done.probes_ref = bf16[8192,64]{1,0:T(8,128)(2,1)} async-done(((bf16[512,64]{1,0:T(8,128)(2,1)}), bf16[8192,64]{1,0:T(8,128)(2,1)}) %all-gather.4.cloned.1.call-update) | async-done | bytes 1048592 | tf_op jit(solution)/shard_map/all_gather | solution.py:214
  54.2 64.7 %all-gather.6.cloned.1.call-done = bf16[8704,256]{1,0:T(8,128)(2,1)} async-done(((bf16[272,256]{1,0:T(8,128)(2,1)}), bf16[8704,256]{1,0:T(8,128)(2,1)}) %all-gather.6.cloned.1.call-update) | async-done | bytes 4456464 | tf_op jit(solution)/shard_map/all_gather | solution.py:213
  118.9 0.0 copy-start
  118.9 1.6 copy-done
  120.5 0.0 copy-start.1
  120.5 0.9 copy-done.1
  121.4 0.0 copy-start.4
  121.4 0.8 copy-done.4
  122.1 0.0 copy-start.8
  122.1 0.7 copy-done.8
  122.8 14.9 %shard_map.122 = (f32[256,128]{1,0:T(8,128)S(1)}, f32[128,128]{1,0:T(8,128)}) custom-call(f32[2]{0:T(128)S(1)} %copy-done.8, bf16[256,256]{1,0:T(8,128)(2,1)S(1)} %get-tuple-element.7.rows_ref, bf16[32,272,256]{2,1,0:T(8,128)(2,1)} %bitcast.6, bf16[8192,64]{1,0:T(8,128)(2,1)S(1)} %copy-done, bf16[512,64]{1,0:T(8,128)(2,1)S(1)} %copy-done.1, ...), custom_call_target="tpu_custom_call" | custom-call | tf_op jit(solution)/shard_map/pallas_call | solution.py:215
  137.7 0.0 all-reduce.2.cloned.1.call-update
  137.7 116.0 %all-reduce.2.cloned.1.call-done.sums_ref = f32[128,128]{1,0:T(8,128)} async-done(((f32[128,128]{1,0:T(8,128)}), f32[128,128]{1,0:T(8,128)}) %all-reduce.2.cloned.1.call-update) | async-done | bytes 65552 | tf_op jit(solution)/shard_map/psum | solution.py:226
  253.7 0.0 copy-start.3
  253.7 0.8 copy-done.3
  254.6 6.5 %shard_map.123 = (f32[64,64]{1,0:T(8,128)}, f32[64,64]{1,0:T(8,128)}, f32[256,64]{1,0:T(8,128)S(1)}) custom-call(f32[256,128]{1,0:T(8,128)S(1)} %get-tuple-element.9.x_ref, f32[128,128]{1,0:T(8,128)S(1)} %copy-done.3), custom_call_target="tpu_custom_call" | custom-call | tf_op jit(solution)/shard_map/pallas_call | solution.py:228
  261.1 0.7 copy.23
Async XLA Ops:
  7.2 47.1 %all-gather.4.cloned.1.call-start = ((), (), s32[]{:S(2)}) async-start(), calls=%async_computation | async-start | bytes 2228224 | tf_op jit(solution)/shard_map/all_gather | solution.py:214
  8.8 110.0 %all-gather.6.cloned.1.call-start = ((), (), s32[]{:S(2)}) async-start(), calls=%async_computation.2 | async-start | bytes 4595712 | tf_op jit(solution)/shard_map/all_gather | solution.py:213
  10.8 0.9 copy-start.2
  11.7 0.8 copy-start.5
  12.4 0.7 copy-start.6
  13.1 0.7 copy-start.7
  26.4 227.3 %all-reduce.2.cloned.1.call-start = ((), (), s32[]{:S(2)}) async-start(), calls=%async_computation.1 | async-start | bytes 131072 | tf_op jit(solution)/shard_map/psum | solution.py:226
  118.9 1.6 copy-start
  120.5 0.9 copy-start.1
  121.4 0.8 copy-start.4
  122.1 0.7 copy-start.8
  253.7 0.8 copy-start.3
Sparse Core Ops, SparseCore 0:
  10.2 44.0 all-gather.3
  57.1 61.7 all-gather.5
  137.9 115.8 all-reduce.1

commit v2 on v1

--- a/solution.py
+++ b/solution.py
@@ -11,6 +11,7 @@
 F32 = jnp.float32
 BF16 = jnp.bfloat16
 EXTRA = 16
+LINE = 4
 HIGH = lax.Precision.HIGHEST
 
 
@@ -77,6 +78,7 @@
     conv_w_ref,
     conv_b_ref,
     inv_len_ref,
+    probes_ref,
     cols_ref,
     rows_ref,
     padded,
@@ -112,35 +114,163 @@
     low = half_sq - high - middle
     order = lax.broadcasted_iota(jnp.int32, (EXTRA, rows), 0)
     tail = jnp.where(order == 0, high, jnp.where(order == 1, middle, jnp.where(order == 2, low, 0.0)))
-    cols_ref[channels:, :] = tail.astype(BF16)
+    cols_ref[channels : channels + EXTRA, :] = tail.astype(BF16)
+    cols_ref[channels + EXTRA :, :] = probes_ref[pl.ds(first, rows), :].astype(F32).T.astype(BF16)
     rows_ref[...] = wide.T.astype(BF16)
 
 
-def apply_kernel(hyper_ref, rows_ref, cols_ref, probes_ref, own_ref, prev_ref, coupling_ref, x_ref, gram_ref, total):
+def apply_kernel(
+    hyper_ref,
+    rows_ref,
+    cols_ref,
+    own_ref,
+    prev_ref,
+    coupling_ref,
+    x_ref,
+    sums_ref,
+    row_blocks,
+    col_blocks,
+    row_halves,
+    totals,
+    partial_out,
+    partial_in,
+    gram_out,
+    gram_in,
+    line_in,
+    gathered,
+    row_send,
+    row_recv,
+    col_send,
+    col_recv,
+    partial_send,
+    partial_recv,
+    gram_send,
+    gram_recv,
+    line_send,
+    line_recv,
+    gather_send,
+    gather_recv,
+):
     rows, channels = rows_ref.shape
-    blocks = cols_ref.shape[0]
-    all_rows = blocks * rows
+    plane = row_blocks.shape[0]
+    line = col_blocks.shape[0]
     width = prev_ref.shape[1]
-    wide = rows_ref[...].astype(F32)
-    row_half = -0.5 * jnp.sum(wide * wide, axis=1, keepdims=True)
+    reps = lax.axis_size("rep")
+    low = plane // reps
+    blk = lax.axis_index("blk")
+    rep = lax.axis_index("rep")
+    my_line = blk // low
+    my_plane = lax.rem(blk, low) * reps + rep
+
+    def plane_id(spot):
+        return {"blk": my_line * low + spot // reps, "rep": lax.rem(spot, reps)}
+
+    def line_id(spot):
+        return {"blk": spot * low + lax.rem(blk, low), "rep": rep}
+
+    def plane_peer(step):
+        return lax.rem(my_plane + step, plane)
+
+    line_peers = [my_line, my_line + 1 - 2 * lax.rem(my_line, 2), lax.rem(my_line + 2, 4), 3 - my_line]
+
+    def copy(src, dst, send_sem, recv_sem, device):
+        return pltpu.make_async_remote_copy(
+            src_ref=src,
+            dst_ref=dst,
+            send_sem=send_sem,
+            recv_sem=recv_sem,
+            device_id=device,
+            device_id_type=pl.DeviceIdType.MESH,
+        )
+
+    def each_plane_peer(action):
+        def body(step, carry):
+            action(step, plane_peer(step))
+            return carry
+
+        lax.fori_loop(1, plane, body, 0)
+
+    barrier = pltpu.get_barrier_semaphore()
+
+    def greet(step, peer):
+        pl.semaphore_signal(barrier, inc=1, device_id=plane_id(peer), device_id_type=pl.DeviceIdType.MESH)
+
+    each_plane_peer(greet)
+    for peer in line_peers[1:]:
+        pl.semaphore_signal(barrier, inc=1, device_id=line_id(peer), device_id_type=pl.DeviceIdType.MESH)
+    pl.semaphore_wait(barrier, plane - 1 + line - 1)
+
+    def col_copy(order, slot, peer):
+        return copy(cols_ref, col_blocks.at[slot], col_send.at[order], col_recv.at[slot], line_id(peer))
+
+    def row_copy(step, slot, peer):
+        return copy(rows_ref, row_blocks.at[slot], row_send.at[step], row_recv.at[slot], plane_id(peer))
+
+    col_copy(1, my_line, line_peers[1]).start()
+    each_plane_peer(lambda step, peer: row_copy(step, my_plane, peer).start())
+    col_copy(2, my_line, line_peers[2]).start()
+    col_copy(3, my_line, line_peers[3]).start()
+    row_blocks[my_plane] = rows_ref[...]
+    col_blocks[my_line] = cols_ref[...]
     amplitude = hyper_ref[0]
-    total[...] = jnp.zeros_like(total)
-
-    def block_step(block, carry):
-        cols = cols_ref[block, :channels, :]
-        tail = cols_ref[block, channels:, :].astype(F32)
-        col_half = jnp.sum(tail, axis=0, keepdims=True)
-        inner = jnp.dot(rows_ref[...], cols, preferred_element_type=F32)
-        exponent = jnp.minimum(inner + (row_half + col_half), 0.0)
-        weights = (amplitude * jnp.exp(exponent)).astype(BF16)
-        start = pl.multiple_of(block * rows, rows)
-        total[...] += jnp.dot(weights, probes_ref[pl.ds(start, rows), :], preferred_element_type=F32)
-        return carry
-
-    lax.fori_loop(0, blocks, block_step, 0)
-    first = pl.multiple_of(lax.axis_index("rep") * rows, rows)
-    own = own_ref[pl.ds(first, rows), :].astype(F32)
-    root = 1.0 / math.sqrt(all_rows)
+
+    def partial_copy(step, slot, peer):
+        return copy(
+            partial_out.at[step], partial_in.at[slot], partial_send.at[step], partial_recv.at[slot], plane_id(peer)
+        )
+
+    def packed(value):
+        return jnp.concatenate([value[: rows // 2, :], value[rows // 2 :, :]], axis=1)
+
+    for order in range(line):
+        source = line_peers[order]
+        if order:
+            col_copy(order, source, source).wait_recv()
+        cols = col_blocks.at[source]
+        col_half = jnp.sum(cols[channels : channels + EXTRA, :].astype(F32), axis=0, keepdims=True)
+        block_probes = cols[channels + EXTRA :, :].astype(F32).T.astype(BF16)
+        last = order == line - 1
+
+        def pair_step(pair, carry, order=order, cols=cols, col_half=col_half, block_probes=block_probes, last=last):
+            for part in range(2):
+                step = 2 * pair + part + (1 if last else 0)
+                spot = plane_peer(step)
+                if order == 0:
+
+                    @pl.when(step > 0)
+                    def _():
+                        row_copy(step, spot, spot).wait_recv()
+
+                    wide = row_blocks[spot].astype(F32)
+                    row_halves[spot] = -0.5 * jnp.sum(wide * wide, axis=1, keepdims=True)
+            for part in range(2):
+                step = 2 * pair + part + (1 if last else 0)
+                spot = plane_peer(step)
+                inner = jnp.dot(row_blocks[spot], cols[:channels, :], preferred_element_type=F32)
+                exponent = jnp.minimum(inner + (row_halves[spot] + col_half), 0.0)
+                weights = (amplitude * jnp.exp(exponent)).astype(BF16)
+                value = jnp.dot(weights, block_probes, preferred_element_type=F32)
+                if order:
+                    value = value + totals[spot]
+                if last:
+                    partial_out[step] = packed(value)
+                else:
+                    totals[spot] = value
+            if last:
+                for part in range(2):
+                    step = 2 * pair + part + 1
+                    spot = plane_peer(step)
+
+                    @pl.when(step < plane)
+                    def _():
+                        partial_copy(step, my_plane, spot).start()
+
+            return carry
+
+        lax.fori_loop(0, plane // 2, pair_step, 0)
+
+    own = own_ref[pl.ds(pl.multiple_of(rep * rows, rows), rows), :].astype(F32)
+    root = 1.0 / math.sqrt(rows * plane * line)
     coupled = lax.dot_general(
         prev_ref[...].astype(F32),
         coupling_ref[...],
@@ -148,10 +278,63 @@
         precision=HIGH,
         preferred_element_type=F32,
     )
+
+    def add_partial(step, total):
+        spot = plane_peer(step)
+        partial_copy(step, spot, spot).wait_recv()
+        return total + partial_in[spot]
+
+    total = lax.fori_loop(1, plane, add_partial, partial_out[plane])
+    applied = jnp.concatenate([total[:, :width], total[:, width:]], axis=0)
     x_ref[:, :width] = own * root
-    x_ref[:, width:] = (total[...] + hyper_ref[1] * own - coupled) * root
+    x_ref[:, width:] = (applied + hyper_ref[1] * own - coupled) * root
     both = x_ref[...]
-    gram_ref[...] = jnp.dot(both.T, both, precision=HIGH, preferred_element_type=F32)
+    gram = jnp.dot(both.T, both, precision=HIGH, preferred_element_type=F32)
+    piece = gram_out.shape[1]
+    for spot in range(plane):
+        gram_out[spot] = gram[spot * piece : (spot + 1) * piece, :]
+
+    def gram_copy(step, target, slot):
+        return copy(gram_out.at[target], gram_in.at[slot], gram_send.at[step], gram_recv.at[slot], plane_id(target))
+
+    each_plane_peer(lambda step, peer: gram_copy(step, peer, my_plane).start())
+
+    def add_gram(step, total):
+        spot = plane_peer(step)
+        gram_copy(step, spot, spot).wait_recv()
+        return total + gram_in[spot]
+
+    line_in[my_line] = lax.fori_loop(1, plane, add_gram, gram_out[my_plane])
+
+    def line_copy(order, slot, peer):
+        return copy(line_in.at[my_line], line_in.at[slot], line_send.at[order], line_recv.at[slot], line_id(peer))
+
+    for order in range(1, line):
+        line_copy(order, my_line, line_peers[order]).start()
+    for order in range(1, line):
+        line_copy(order, line_peers[order], line_peers[order]).wait_recv()
+    gathered[my_plane] = (line_in[0] + line_in[1]) + (line_in[2] + line_in[3])
+
+    def gather_copy(step, slot, peer):
+        return copy(
+            gathered.at[my_plane], gathered.at[slot], gather_send.at[step], gather_recv.at[slot], plane_id(peer)
+        )
+
+    each_plane_peer(lambda step, peer: gather_copy(step, my_plane, peer).start())
+    each_plane_peer(lambda step, peer: gather_copy(step, peer, peer).wait_recv())
+    for spot in range(plane):
+        sums_ref[spot * piece : (spot + 1) * piece, :] = gathered[spot]
+    for order in range(1, line):
+        col_copy(order, my_line, line_peers[order]).wait_send()
+        line_copy(order, my_line, line_peers[order]).wait_send()
+
+    def drain(step, peer):
+        row_copy(step, my_plane, peer).wait_send()
+        partial_copy(step, my_plane, peer).wait_send()
+        gram_copy(step, peer, my_plane).wait_send()
+        gather_copy(step, my_plane, peer).wait_send()
+
+    each_plane_peer(drain)
 
 
 def finish_kernel(root, x_ref, sums_ref, a_ref, r_ref, next_ref):
@@ -195,10 +378,10 @@
     cols, own_rows = pl.pallas_call(
         feature_kernel,
         out_shape=(
-            jax.ShapeDtypeStruct((channels + EXTRA, rows), BF16),
+            jax.ShapeDtypeStruct((channels + EXTRA + width, rows), BF16),
             jax.ShapeDtypeStruct((rows, channels), BF16),
         ),
-        in_specs=[VMEM] * 6,
+        in_specs=[VMEM] * 7,
         out_specs=(VMEM, VMEM),
         scratch_shapes=[
             pltpu.VMEM((rows, 128), jnp.int32),
@@ -209,22 +392,48 @@
             pltpu.VMEM((channels, rows), F32),
         ],
         compiler_params=PARAMS,
-    )(tokens, lengths.reshape(1, -1), embed, conv_w, conv_b.reshape(1, -1), inv_len.reshape(-1, 1))
-    all_cols = lax.all_gather(cols, ("blk", "rep"), axis=0)
-    all_probes = lax.all_gather(probes, "blk", axis=0, tiled=True)
-    pair, gram = pl.pallas_call(
+    )(tokens, lengths.reshape(1, -1), embed, conv_w, conv_b.reshape(1, -1), inv_len.reshape(-1, 1), probes)
+    line = LINE
+    plane = lax.axis_size("blk") // line * lax.axis_size("rep")
+    piece = 2 * width // plane
+    dma = pltpu.SemaphoreType.DMA
+    pair, sums = pl.pallas_call(
         apply_kernel,
         out_shape=(
             jax.ShapeDtypeStruct((rows, 2 * width), F32),
             jax.ShapeDtypeStruct((2 * width, 2 * width), F32),
         ),
-        in_specs=[SMEM] + [VMEM] * 6,
+        in_specs=[SMEM] + [VMEM] * 5,
         out_specs=(VMEM, VMEM),
-        scratch_shapes=[pltpu.VMEM((rows, width), F32)],
-        compiler_params=PARAMS,
-    )(hyper, own_rows, all_cols, all_probes, probes, prev_probes, coupling)
-    sums = lax.psum(gram, ("blk", "rep"))
-    root = math.sqrt(all_probes.shape[0])
+        scratch_shapes=[
+            pltpu.VMEM((plane, rows, channels), BF16),
+            pltpu.VMEM((line, channels + EXTRA + width, rows), BF16),
+            pltpu.VMEM((plane, rows, 1), F32),
+            pltpu.VMEM((plane, rows, width), F32),
+            pltpu.VMEM((plane + 1, rows // 2, 2 * width), F32),
+            pltpu.VMEM((plane, rows // 2, 2 * width), F32),
+            pltpu.VMEM((plane, piece, 2 * width), F32),
+            pltpu.VMEM((plane, piece, 2 * width), F32),
+            pltpu.VMEM((line, piece, 2 * width), F32),
+            pltpu.VMEM((plane, piece, 2 * width), F32),
+            dma((plane,)),
+            dma((plane,)),
+            dma((line,)),
+            dma((line,)),
+            dma((plane,)),
+            dma((plane,)),
+            dma((plane,)),
+            dma((plane,)),
+            dma((line,)),
+            dma((line,)),
+            dma((plane,)),
+            dma((plane,)),
+        ],
+        compiler_params=pltpu.CompilerParams(
+            vmem_limit_bytes=48 * 1024 * 1024, collective_id=0, has_side_effects=True
+        ),
+    )(hyper, own_rows, cols, probes, prev_probes, coupling)
+    root = math.sqrt(rows * plane * line)
     return pl.pallas_call(
         functools.partial(finish_kernel, root),
         out_shape=(

time: 270 us -> 68.9 us (0.26)
  waiting for transfers between devices: 208 us -> 0 us
  Pallas kernels: 34 us -> 64 us
  between operations: 13.8 us -> 0.76 us
  local copies, waits for them, and re-layouts: 12.8 us -> 3.93 us
    psum x1 -> x0, waiting for transfers between devices: 116 us -> none  [per_device(): sums = lax.psum(gram, ('blk', 'rep'))]
    all_gather x2 -> x0, waiting for transfers between devices: 91.6 us -> none  [the longest x1 64.7 us: per_device(): all_cols = lax.all_gather(cols, ('blk', 'rep'), axis=0)]
    pallas_call x1, Pallas kernels: 14.9 us -> 45.5 us  [per_device(): pl.pallas_call(apply_kernel, out_shape=(jax.ShapeDtypeStruct((rows, 2 * w...]
    unnamed x21, local copies, waits for them, and re-layouts: 11.3 us -> 3.08 us
  transfers between devices with their start and end apart: 3 -> 0, of which waited for: 3 -> 0; matrix products, arithmetic and copies ran while one was open for 1% -> 0% of each run, Pallas kernels for 5% -> 0%
where the time goes in v2:
time: 68.9 us; the launch traced here: 68.7 us
  Pallas kernels  64 us (93%)
  local copies, waits for them, and re-layouts  3.93 us (6%)
  between operations  0.76 us (1%)
    pallas_call x1, Pallas kernels, per_device(): pl.pallas_call(apply_kernel, out_shape=(jax.ShapeDtypeStruct((rows, 2 * w...  45.5 us
    pallas_call x1, Pallas kernels, per_device(): pl.pallas_call(feature_kernel, out_shape=(jax.ShapeDtypeStruct((channels...  12 us
    pallas_call x1, Pallas kernels, per_device(): pl.pallas_call(functools.partial(finish_kernel, root), out_shape=(jax.Sha...  6.51 us
    unnamed x21, local copies, waits for them, and re-layouts  3.08 us

profile of v2, /device:TPU:0, one launch (start us, length us, event | category | flops | bytes accessed | tf_op | source)
XLA Modules:
  0.0 68.7 jit_solution(13086633957904806485)
XLA Ops:
  0.6 0.0 copy-start.6
  0.6 1.0 %copy.20.probes_ref.own_ref = bf16[512,64]{1,0:T(8,128)(2,1)S(1)} copy(bf16[512,64]{0,1:T(8,128)(2,1)} %param.17) | data formatting | bytes 131072 | tf_op args[7]
  1.6 0.0 copy-done.6
  1.6 0.0 copy-start.8
  1.7 0.0 copy-start.2
  1.7 0.1 copy.18.tokens_ref
  1.8 0.0 copy-start
  1.8 0.5 copy-done.8
  2.3 0.1 copy.19.inv_len_ref
  2.5 0.0 copy-start.3
  2.5 0.0 copy-start.4
  2.5 0.0 copy-done.2
  2.5 0.2 copy-done
  2.7 0.5 copy-done.3
  3.2 0.0 copy-done.4
  3.2 0.0 copy-start.7
  3.2 12.0 %shard_map.121 = (bf16[336,256]{1,0:T(8,128)(2,1)S(1)}, bf16[256,256]{1,0:T(8,128)(2,1)S(1)}) custom-call(s32[512,69]{1,0:T(8,128)S(1)} %copy.18.tokens_ref, s32[1,512]{1,0:T(1,128)S(1)} %bitcast.3, bf16[64,256]{1,0:T(8,128)(2,1)S(1)} %copy-done.2, bf16[7,32,256]{2,1,0:T(8,128)(2,1)S(1)} %copy-done, f32[1,256]{1,0:T(1,128)S(1)} %bitcast.4, ...), custom_call_target="tpu_custom_call" | custom-call | tf_op jit(solution)/shard_map/pallas_call | solution.py:378
  15.2 0.0 copy-done.7
  15.2 0.0 copy-start.1
  15.2 0.0 copy-start.5
  15.2 0.1 copy.22.prev_ref
  15.4 0.6 copy-done.1
  16.0 0.0 copy-done.5
  16.0 45.5 %shard_map.122 = (f32[256,128]{1,0:T(8,128)S(1)}, f32[128,128]{1,0:T(8,128)S(1)}) custom-call(f32[2]{0:T(128)S(1)} %copy-done.5, bf16[256,256]{1,0:T(8,128)(2,1)S(1)} %get-tuple-element.7.rows_ref, bf16[336,256]{1,0:T(8,128)(2,1)S(1)} %get-tuple-element.8.cols_ref, bf16[512,64]{1,0:T(8,128)(2,1)S(1)} %copy.20.probes_ref.own_ref, ...), custom_call_target="tpu_custom_call" | custom-call | tf_op jit(solution)/shard_map/pallas_call | solution.py:400
  61.5 6.5 %shard_map.123 = (f32[64,64]{1,0:T(8,128)}, f32[64,64]{1,0:T(8,128)}, f32[256,64]{1,0:T(8,128)S(1)}) custom-call(f32[256,128]{1,0:T(8,128)S(1)} %get-tuple-element.9.x_ref, f32[128,128]{1,0:T(8,128)S(1)} %get-tuple-element.10.sums_ref), custom_call_target="tpu_custom_call" | custom-call | tf_op jit(solution)/shard_map/pallas_call | solution.py:437
  68.0 0.7 %copy.23 = f32[256,64]{0,1:T(8,128)} copy(f32[256,64]{1,0:T(8,128)S(1)} %get-tuple-element.16) | data formatting | bytes 131072 | tf_op jit(solution)/shard_map/pallas_call | solution.py:437
Async XLA Ops:
  0.6 1.0 %copy-start.6 = (s32[512,69]{0,1:T(8,128)S(1)}, s32[512,69]{0,1:T(8,128)}, u32[]{:S(2)}) copy-start(s32[512,69]{0,1:T(8,128)} %param.10) | copy-start | bytes 423940
  1.6 0.7 copy-start.8
  1.7 0.8 %copy-start.2 = (bf16[64,256]{1,0:T(8,128)(2,1)S(1)}, bf16[64,256]{1,0:T(8,128)(2,1)}, u32[]{:S(2)}) copy-start(bf16[64,256]{1,0:T(8,128)(2,1)} %embed_ref.1) | copy-start | bytes 98308
  1.8 0.9 %copy-start = (bf16[7,32,256]{2,1,0:T(8,128)(2,1)S(1)}, bf16[7,32,256]{2,1,0:T(8,128)(2,1)}, u32[]{:S(2)}) copy-start(bf16[7,32,256]{2,1,0:T(8,128)(2,1)} %conv_w_ref.1) | copy-start | bytes 344068
  2.5 0.7 %copy-start.3 = (s32[512]{0:T(512)S(1)}, s32[512]{0:T(512)}, u32[]{:S(2)}) copy-start(s32[512]{0:T(512)} %param.11) | copy-start | bytes 6148
  2.5 0.7 %copy-start.4 = (f32[256]{0:T(256)S(1)}, f32[256]{0:T(256)}, u32[]{:S(2)}) copy-start(f32[256]{0:T(256)} %param.14) | copy-start | bytes 3076
  3.2 12.0 %copy-start.7 = (bf16[256,64]{0,1:T(8,128)(2,1)S(1)}, bf16[256,64]{0,1:T(8,128)(2,1)}, u32[]{:S(2)}) copy-start(bf16[256,64]{0,1:T(8,128)(2,1)} %param.18) | copy-start | bytes 98308
  15.2 0.8 %copy-start.1 = (f32[64,64]{1,0:T(8,128)S(1)}, f32[64,64]{1,0:T(8,128)}, u32[]{:S(2)}) copy-start(f32[64,64]{1,0:T(8,128)} %coupling_ref.1) | copy-start | bytes 49156
  15.2 0.8 %copy-start.5 = (f32[2]{0:T(128)S(1)}, f32[2]{0:T(128)}, u32[]{:S(2)}) copy-start(f32[2]{0:T(128)} %hyper_ref.1) | copy-start | bytes 28

commit v3 on v2

--- a/solution.py
+++ b/solution.py
@@ -140,8 +140,11 @@
     gathered,
     row_send,
     row_recv,
-    col_send,
+    up_send,
+    down_send,
     col_recv,
+    side_send,
+    side_recv,
     partial_send,
     partial_recv,
     gram_send,
@@ -152,26 +155,38 @@
     gather_recv,
 ):
     rows, channels = rows_ref.shape
-    plane = row_blocks.shape[0]
+    mates = row_blocks.shape[0]
     line = col_blocks.shape[0]
+    plane = gram_out.shape[0]
     width = prev_ref.shape[1]
     reps = lax.axis_size("rep")
     low = plane // reps
     blk = lax.axis_index("blk")
     rep = lax.axis_index("rep")
-    my_line = blk // low
+    core = lax.rem(blk, 2)
+    other = 1 - core
+    mine = blk // low
     my_plane = lax.rem(blk, low) * reps + rep
+    my_mate = (lax.rem(blk, low) // 2) * reps + rep
 
     def plane_id(spot):
-        return {"blk": my_line * low + spot // reps, "rep": lax.rem(spot, reps)}
+        return {"blk": mine * low + spot // reps, "rep": lax.rem(spot, reps)}
+
+    def mate_id(spot):
+        return {"blk": mine * low + (spot // reps) * 2 + core, "rep": lax.rem(spot, reps)}
 
     def line_id(spot):
         return {"blk": spot * low + lax.rem(blk, low), "rep": rep}
 
+    sibling = {"blk": blk + 1 - 2 * core, "rep": rep}
+
     def plane_peer(step):
         return lax.rem(my_plane + step, plane)
 
-    line_peers = [my_line, my_line + 1 - 2 * lax.rem(my_line, 2), lax.rem(my_line + 2, 4), 3 - my_line]
+    def mate_peer(step):
+        return lax.rem(my_mate + step, mates)
+
+    line_peers = [mine, mine + 1 - 2 * lax.rem(mine, 2), lax.rem(mine + 2, 4), 3 - mine]
 
     def copy(src, dst, send_sem, recv_sem, device):
         return pltpu.make_async_remote_copy(
@@ -190,6 +205,13 @@
 
         lax.fori_loop(1, plane, body, 0)
 
+    def each_mate(action):
+        def body(step, carry):
+            action(step, mate_peer(step))
+            return carry
+
+        lax.fori_loop(1, mates, body, 0)
+
     barrier = pltpu.get_barrier_semaphore()
 
     def greet(step, peer):
@@ -200,42 +222,81 @@
         pl.semaphore_signal(barrier, inc=1, device_id=line_id(peer), device_id_type=pl.DeviceIdType.MESH)
     pl.semaphore_wait(barrier, plane - 1 + line - 1)
 
-    def col_copy(order, slot, peer):
-        return copy(cols_ref, col_blocks.at[slot], col_send.at[order], col_recv.at[slot], line_id(peer))
+    def up_copy(slot, src=None):
+        src = col_blocks.at[slot, core] if src is None else src
+        return copy(src, col_blocks.at[slot, core], up_send.at[slot], col_recv.at[slot], line_id(mine + 1))
+
+    def down_copy(slot, src=None):
+        src = col_blocks.at[slot, core] if src is None else src
+        return copy(src, col_blocks.at[slot, core], down_send.at[slot], col_recv.at[slot], line_id(mine - 1))
+
+    def side_copy(slot, lane, src=None):
+        src = col_blocks.at[slot, lane] if src is None else src
+        return copy(src, col_blocks.at[slot, lane], side_send.at[slot], side_recv.at[slot], sibling)
 
     def row_copy(step, slot, peer):
-        return copy(rows_ref, row_blocks.at[slot], row_send.at[step], row_recv.at[slot], plane_id(peer))
-
-    col_copy(1, my_line, line_peers[1]).start()
-    each_plane_peer(lambda step, peer: row_copy(step, my_plane, peer).start())
-    col_copy(2, my_line, line_peers[2]).start()
-    col_copy(3, my_line, line_peers[3]).start()
-    row_blocks[my_plane] = rows_ref[...]
-    col_blocks[my_line] = cols_ref[...]
+        return copy(rows_ref, row_blocks.at[slot], row_send.at[step], row_recv.at[slot], mate_id(peer))
+
+    @pl.when(mine < line - 1)
+    def _():
+        up_copy(mine, cols_ref).start()
+
+    @pl.when(mine > 0)
+    def _():
+        down_copy(mine, cols_ref).start()
+
+    each_mate(lambda step, peer: row_copy(step, my_mate, peer).start())
+    side_copy(mine, core, cols_ref).start()
+    row_blocks[my_mate] = rows_ref[...]
+    col_blocks[mine, core] = cols_ref[...]
     amplitude = hyper_ref[0]
+
+    def pass_on(distance):
+        @pl.when(mine >= distance)
+        def _():
+            slot = mine - distance
+            up_copy(slot).wait_recv()
+
+            @pl.when(mine < line - 1)
+            def _():
+                up_copy(slot).start()
+
+            side_copy(slot, core).start()
+
+        @pl.when(mine + distance < line)
+        def _():
+            slot = mine + distance
+            down_copy(slot).wait_recv()
+
+            @pl.when(mine > 0)
+            def _():
+                down_copy(slot).start()
+
+            side_copy(slot, core).start()
 
     def partial_copy(step, slot, peer):
         return copy(
-            partial_out.at[step], partial_in.at[slot], partial_send.at[step], partial_recv.at[slot], plane_id(peer)
+            partial_out.at[step], partial_in.at[slot], partial_send.at[step], partial_recv.at[slot], mate_id(peer)
         )
 
     def packed(value):
         return jnp.concatenate([value[: rows // 2, :], value[rows // 2 :, :]], axis=1)
 
-    for order in range(line):
-        source = line_peers[order]
-        if order:
-            col_copy(order, source, source).wait_recv()
-        cols = col_blocks.at[source]
-        col_half = jnp.sum(cols[channels : channels + EXTRA, :].astype(F32), axis=0, keepdims=True)
-        block_probes = cols[channels + EXTRA :, :].astype(F32).T.astype(BF16)
+    def column_pass(source, order):
+        side_copy(source, other).wait_recv()
+        parts = []
+        for lane in range(2):
+            cols = col_blocks.at[source, lane]
+            col_half = jnp.sum(cols[channels : channels + EXTRA, :].astype(F32), axis=0, keepdims=True)
+            block_probes = cols[channels + EXTRA :, :].astype(F32).T.astype(BF16)
+            parts.append((cols, col_half, block_probes))
         last = order == line - 1
 
-        def pair_step(pair, carry, order=order, cols=cols, col_half=col_half, block_probes=block_probes, last=last):
-            for part in range(2):
-                step = 2 * pair + part + (1 if last else 0)
-                spot = plane_peer(step)
-                if order == 0:
+        def pair_step(pair, carry):
+            steps = [2 * pair + part + (1 if last else 0) for part in range(2)]
+            if order == 0:
+                for step in steps:
+                    spot = mate_peer(step)
 
                     @pl.when(step > 0)
                     def _():
@@ -243,31 +304,41 @@
 
                     wide = row_blocks[spot].astype(F32)
                     row_halves[spot] = -0.5 * jnp.sum(wide * wide, axis=1, keepdims=True)
-            for part in range(2):
-                step = 2 * pair + part + (1 if last else 0)
-                spot = plane_peer(step)
-                inner = jnp.dot(row_blocks[spot], cols[:channels, :], preferred_element_type=F32)
-                exponent = jnp.minimum(inner + (row_halves[spot] + col_half), 0.0)
-                weights = (amplitude * jnp.exp(exponent)).astype(BF16)
-                value = jnp.dot(weights, block_probes, preferred_element_type=F32)
-                if order:
-                    value = value + totals[spot]
+            for step in steps:
+                spot = mate_peer(step)
+                value = None if order == 0 else totals[spot]
+                for cols, col_half, block_probes in parts:
+                    inner = jnp.dot(row_blocks[spot], cols[:channels, :], preferred_element_type=F32)
+                    exponent = jnp.minimum(inner + (row_halves[spot] + col_half), 0.0)
+                    weights = (amplitude * jnp.exp(exponent)).astype(BF16)
+                    term = jnp.dot(weights, block_probes, preferred_element_type=F32)
+                    value = term if value is None else value + term
                 if last:
                     partial_out[step] = packed(value)
                 else:
                     totals[spot] = value
             if last:
-                for part in range(2):
-                    step = 2 * pair + part + 1
-                    spot = plane_peer(step)
-
-                    @pl.when(step < plane)
+                for step in steps:
+                    spot = mate_peer(step)
+
+                    @pl.when(step < mates)
                     def _():
-                        partial_copy(step, my_plane, spot).start()
+                        partial_copy(step, my_mate, spot).start()
 
             return carry
 
-        lax.fori_loop(0, plane // 2, pair_step, 0)
+        lax.fori_loop(0, mates // 2, pair_step, 0)
+
+    second = jnp.where(mine == 0, 1, mine - 1)
+    third = jnp.where(mine < 2, 2, jnp.where(mine == 2, 3, 1))
+    fourth = jnp.where(mine < 2, 3, 0)
+    column_pass(mine, 0)
+    pass_on(1)
+    column_pass(second, 1)
+    pass_on(2)
+    column_pass(third, 2)
+    pass_on(3)
+    column_pass(fourth, 3)
 
     own = own_ref[pl.ds(pl.multiple_of(rep * rows, rows), rows), :].astype(F32)
     root = 1.0 / math.sqrt(rows * plane * line)
@@ -280,11 +351,11 @@
     )
 
     def add_partial(step, total):
-        spot = plane_peer(step)
+        spot = mate_peer(step)
         partial_copy(step, spot, spot).wait_recv()
         return total + partial_in[spot]
 
-    total = lax.fori_loop(1, plane, add_partial, partial_out[plane])
+    total = lax.fori_loop(1, mates, add_partial, partial_out[mates])
     applied = jnp.concatenate([total[:, :width], total[:, width:]], axis=0)
     x_ref[:, :width] = own * root
     x_ref[:, width:] = (applied + hyper_ref[1] * own - coupled) * root
@@ -304,13 +375,13 @@
         gram_copy(step, spot, spot).wait_recv()
         return total + gram_in[spot]
 
-    line_in[my_line] = lax.fori_loop(1, plane, add_gram, gram_out[my_plane])
+    line_in[mine] = lax.fori_loop(1, plane, add_gram, gram_out[my_plane])
 
     def line_copy(order, slot, peer):
-        return copy(line_in.at[my_line], line_in.at[slot], line_send.at[order], line_recv.at[slot], line_id(peer))
+        return copy(line_in.at[mine], line_in.at[slot], line_send.at[order], line_recv.at[slot], line_id(peer))
 
     for order in range(1, line):
-        line_copy(order, my_line, line_peers[order]).start()
+        line_copy(order, mine, line_peers[order]).start()
     for order in range(1, line):
         line_copy(order, line_peers[order], line_peers[order]).wait_recv()
     gathered[my_plane] = (line_in[0] + line_in[1]) + (line_in[2] + line_in[3])
@@ -325,15 +396,27 @@
     for spot in range(plane):
         sums_ref[spot * piece : (spot + 1) * piece, :] = gathered[spot]
     for order in range(1, line):
-        col_copy(order, my_line, line_peers[order]).wait_send()
-        line_copy(order, my_line, line_peers[order]).wait_send()
+        line_copy(order, mine, line_peers[order]).wait_send()
+    for slot in range(line):
+        side_copy(slot, core).wait_send()
+
+        @pl.when((mine >= slot) & (mine < line - 1))
+        def _(slot=slot):
+            up_copy(slot).wait_send()
+
+        @pl.when((mine <= slot) & (mine > 0))
+        def _(slot=slot):
+            down_copy(slot).wait_send()
+
+    def drain_mate(step, peer):
+        row_copy(step, my_mate, peer).wait_send()
+        partial_copy(step, my_mate, peer).wait_send()
 
     def drain(step, peer):
-        row_copy(step, my_plane, peer).wait_send()
-        partial_copy(step, my_plane, peer).wait_send()
         gram_copy(step, peer, my_plane).wait_send()
         gather_copy(step, my_plane, peer).wait_send()
 
+    each_mate(drain_mate)
     each_plane_peer(drain)
 
 
@@ -395,6 +478,7 @@
     )(tokens, lengths.reshape(1, -1), embed, conv_w, conv_b.reshape(1, -1), inv_len.reshape(-1, 1), probes)
     line = LINE
     plane = lax.axis_size("blk") // line * lax.axis_size("rep")
+    mates = plane // 2
     piece = 2 * width // plane
     dma = pltpu.SemaphoreType.DMA
     pair, sums = pl.pallas_call(
@@ -406,22 +490,25 @@
         in_specs=[SMEM] + [VMEM] * 5,
         out_specs=(VMEM, VMEM),
         scratch_shapes=[
-            pltpu.VMEM((plane, rows, channels), BF16),
-            pltpu.VMEM((line, channels + EXTRA + width, rows), BF16),
-            pltpu.VMEM((plane, rows, 1), F32),
-            pltpu.VMEM((plane, rows, width), F32),
-            pltpu.VMEM((plane + 1, rows // 2, 2 * width), F32),
-            pltpu.VMEM((plane, rows // 2, 2 * width), F32),
+            pltpu.VMEM((mates, rows, channels), BF16),
+            pltpu.VMEM((line, 2, channels + EXTRA + width, rows), BF16),
+            pltpu.VMEM((mates, rows, 1), F32),
+            pltpu.VMEM((mates, rows, width), F32),
+            pltpu.VMEM((mates + 1, rows // 2, 2 * width), F32),
+            pltpu.VMEM((mates, rows // 2, 2 * width), F32),
             pltpu.VMEM((plane, piece, 2 * width), F32),
             pltpu.VMEM((plane, piece, 2 * width), F32),
             pltpu.VMEM((line, piece, 2 * width), F32),
             pltpu.VMEM((plane, piece, 2 * width), F32),
-            dma((plane,)),
-            dma((plane,)),
-            dma((line,)),
-            dma((line,)),
-            dma((plane,)),
-            dma((plane,)),
+            dma((mates,)),
+            dma((mates,)),
+            dma((line,)),
+            dma((line,)),
+            dma((line,)),
+            dma((line,)),
+            dma((line,)),
+            dma((mates,)),
+            dma((mates,)),
             dma((plane,)),
             dma((plane,)),
             dma((line,)),

time: 68.9 us -> 66.1 us (0.959)
  Pallas kernels: 64 us -> 61.1 us
    pallas_call x1, Pallas kernels: 45.5 us -> 42.6 us  [per_device(): pl.pallas_call(apply_kernel, out_shape=(jax.ShapeDtypeStruct((rows, 2 * w...]
where the time goes in v3:
time: 66.1 us; the launch traced here: 65.8 us
  Pallas kernels  61.1 us (92%)
  local copies, waits for them, and re-layouts  3.93 us (6%)
  between operations  0.76 us (1%)
    pallas_call x1, Pallas kernels, per_device(): pl.pallas_call(apply_kernel, out_shape=(jax.ShapeDtypeStruct((rows, 2 * w...  42.6 us
    pallas_call x1, Pallas kernels, per_device(): pl.pallas_call(feature_kernel, out_shape=(jax.ShapeDtypeStruct((channels...  12 us
    pallas_call x1, Pallas kernels, per_device(): pl.pallas_call(functools.partial(finish_kernel, root), out_shape=(jax.Sha...  6.51 us
    unnamed x21, local copies, waits for them, and re-layouts  3.08 us

profile of v3, /device:TPU:0, one launch (start us, length us, event | category | flops | bytes accessed | tf_op | source)
XLA Modules:
  0.0 65.8 jit_solution(1764173866324951668)
XLA Ops:
  0.6 0.0 copy-start.6
  0.6 1.0 %copy.20.probes_ref.own_ref = bf16[512,64]{1,0:T(8,128)(2,1)S(1)} copy(bf16[512,64]{0,1:T(8,128)(2,1)} %param.17) | data formatting | bytes 131072 | tf_op args[7]
  1.6 0.0 copy-done.6
  1.6 0.0 copy-start.8
  1.7 0.0 copy-start.2
  1.7 0.1 copy.18.tokens_ref
  1.8 0.0 copy-start
  1.8 0.5 copy-done.8
  2.3 0.1 copy.19.inv_len_ref
  2.5 0.0 copy-start.3
  2.5 0.0 copy-start.4
  2.5 0.0 copy-done.2
  2.5 0.2 copy-done
  2.7 0.5 copy-done.3
  3.2 0.0 copy-done.4
  3.2 0.0 copy-start.7
  3.2 12.0 %shard_map.121 = (bf16[336,256]{1,0:T(8,128)(2,1)S(1)}, bf16[256,256]{1,0:T(8,128)(2,1)S(1)}) custom-call(s32[512,69]{1,0:T(8,128)S(1)} %copy.18.tokens_ref, s32[1,512]{1,0:T(1,128)S(1)} %bitcast.3, bf16[64,256]{1,0:T(8,128)(2,1)S(1)} %copy-done.2, bf16[7,32,256]{2,1,0:T(8,128)(2,1)S(1)} %copy-done, f32[1,256]{1,0:T(1,128)S(1)} %bitcast.4, ...), custom_call_target="tpu_custom_call" | custom-call | tf_op jit(solution)/shard_map/pallas_call | solution.py:461
  15.2 0.0 copy-done.7
  15.2 0.0 copy-start.1
  15.2 0.0 copy-start.5
  15.2 0.1 copy.22.prev_ref
  15.4 0.6 copy-done.1
  16.0 0.0 copy-done.5
  16.0 42.6 %shard_map.122 = (f32[256,128]{1,0:T(8,128)S(1)}, f32[128,128]{1,0:T(8,128)S(1)}) custom-call(f32[2]{0:T(128)S(1)} %copy-done.5, bf16[256,256]{1,0:T(8,128)(2,1)S(1)} %get-tuple-element.7.rows_ref, bf16[336,256]{1,0:T(8,128)(2,1)S(1)} %get-tuple-element.8.cols_ref, bf16[512,64]{1,0:T(8,128)(2,1)S(1)} %copy.20.probes_ref.own_ref, ...), custom_call_target="tpu_custom_call" | custom-call | tf_op jit(solution)/shard_map/pallas_call | solution.py:484
  58.6 6.5 %shard_map.123 = (f32[64,64]{1,0:T(8,128)}, f32[64,64]{1,0:T(8,128)}, f32[256,64]{1,0:T(8,128)S(1)}) custom-call(f32[256,128]{1,0:T(8,128)S(1)} %get-tuple-element.9.x_ref, f32[128,128]{1,0:T(8,128)S(1)} %get-tuple-element.10.sums_ref), custom_call_target="tpu_custom_call" | custom-call | tf_op jit(solution)/shard_map/pallas_call | solution.py:524
  65.1 0.7 %copy.23 = f32[256,64]{0,1:T(8,128)} copy(f32[256,64]{1,0:T(8,128)S(1)} %get-tuple-element.16) | data formatting | bytes 131072 | tf_op jit(solution)/shard_map/pallas_call | solution.py:524
Async XLA Ops:
  0.6 1.0 %copy-start.6 = (s32[512,69]{0,1:T(8,128)S(1)}, s32[512,69]{0,1:T(8,128)}, u32[]{:S(2)}) copy-start(s32[512,69]{0,1:T(8,128)} %param.10) | copy-start | bytes 423940
  1.6 0.7 %copy-start.8 = (f32[256]{0:T(256)S(1)}, f32[256]{0:T(256)}, u32[]{:S(2)}) copy-start(f32[256]{0:T(256)} %param.15) | copy-start | bytes 3076
  1.7 0.8 %copy-start.2 = (bf16[64,256]{1,0:T(8,128)(2,1)S(1)}, bf16[64,256]{1,0:T(8,128)(2,1)}, u32[]{:S(2)}) copy-start(bf16[64,256]{1,0:T(8,128)(2,1)} %embed_ref.1) | copy-start | bytes 98308
  1.8 0.9 %copy-start = (bf16[7,32,256]{2,1,0:T(8,128)(2,1)S(1)}, bf16[7,32,256]{2,1,0:T(8,128)(2,1)}, u32[]{:S(2)}) copy-start(bf16[7,32,256]{2,1,0:T(8,128)(2,1)} %conv_w_ref.1) | copy-start | bytes 344068
  2.5 0.7 %copy-start.3 = (s32[512]{0:T(512)S(1)}, s32[512]{0:T(512)}, u32[]{:S(2)}) copy-start(s32[512]{0:T(512)} %param.11) | copy-start | bytes 6148
  2.5 0.7 %copy-start.4 = (f32[256]{0:T(256)S(1)}, f32[256]{0:T(256)}, u32[]{:S(2)}) copy-start(f32[256]{0:T(256)} %param.14) | copy-start | bytes 3076
  3.2 12.0 %copy-start.7 = (bf16[256,64]{0,1:T(8,128)(2,1)S(1)}, bf16[256,64]{0,1:T(8,128)(2,1)}, u32[]{:S(2)}) copy-start(bf16[256,64]{0,1:T(8,128)(2,1)} %param.18) | copy-start | bytes 98308
  15.2 0.8 %copy-start.1 = (f32[64,64]{1,0:T(8,128)S(1)}, f32[64,64]{1,0:T(8,128)}, u32[]{:S(2)}) copy-start(f32[64,64]{1,0:T(8,128)} %coupling_ref.1) | copy-start | bytes 49156
  15.2 0.8 %copy-start.5 = (f32[2]{0:T(128)S(1)}, f32[2]{0:T(128)}, u32[]{:S(2)}) copy-start(f32[2]{0:T(128)} %hyper_ref.1) | copy-start | bytes 28

commit v4 on v3

--- a/solution.py
+++ b/solution.py
@@ -12,6 +12,8 @@
 BF16 = jnp.bfloat16
 EXTRA = 16
 LINE = 4
+GROUP = 4
+PANEL = 4
 HIGH = lax.Precision.HIGHEST
 
 
@@ -52,18 +54,23 @@
     pooled[...] = jnp.zeros_like(pooled)
     root = math.sqrt(2.0 / math.pi)
 
-    def position_step(position, carry):
-        start = pl.multiple_of(position * (2 * vocab), 2 * vocab)
-        window = onehot[pl.ds(start, taps * vocab), :]
-        preact = jnp.dot(table_hi[...], window, preferred_element_type=F32)
-        preact = preact + jnp.dot(table_lo[...], window, preferred_element_type=F32)
-        inner = preact * (root + (root * 0.044715) * (preact * preact))
-        half = jnp.where(position < counts, 0.5, 0.0)
-        weighted = preact * half
-        pooled[...] += weighted + weighted * jnp.tanh(inner)
+    def position_step(group, carry):
+        total = None
+        for part in range(GROUP):
+            position = group * GROUP + part
+            start = pl.multiple_of(position * (2 * vocab), 2 * vocab)
+            window = onehot[pl.ds(start, taps * vocab), :]
+            preact = jnp.dot(table_hi[...], window, preferred_element_type=F32)
+            preact = preact + jnp.dot(table_lo[...], window, preferred_element_type=F32)
+            inner = preact * (root + (root * 0.044715) * (preact * preact))
+            half = jnp.where(position < counts, 0.5, 0.0)
+            weighted = preact * half
+            term = weighted + weighted * jnp.tanh(inner)
+            total = term if total is None else total + term
+        pooled[...] += total
         return carry
 
-    lax.fori_loop(0, positions, position_step, 0)
+    lax.fori_loop(0, positions // GROUP, position_step, 0)
     mean_pool = pooled[...] / counts.astype(F32)
     centered = mean_pool - jnp.mean(mean_pool, axis=0, keepdims=True)
     variance = jnp.mean(centered * centered, axis=0, keepdims=True)
@@ -292,8 +299,10 @@
             parts.append((cols, col_half, block_probes))
         last = order == line - 1
 
+        group = 1 if order == 0 else 2
+
         def pair_step(pair, carry):
-            steps = [2 * pair + part + (1 if last else 0) for part in range(2)]
+            steps = [group * pair + part + (1 if last else 0) for part in range(group)]
             if order == 0:
                 for step in steps:
                     spot = mate_peer(step)
@@ -327,7 +336,7 @@
 
             return carry
 
-        lax.fori_loop(0, mates // 2, pair_step, 0)
+        lax.fori_loop(0, mates // group, pair_step, 0)
 
     second = jnp.where(mine == 0, 1, mine - 1)
     third = jnp.where(mine < 2, 2, jnp.where(mine == 2, 3, 1))
@@ -434,13 +443,28 @@
     eye = jnp.where(row == col, 1.0, 0.0)
     work = jnp.concatenate([gram, eye], axis=1)
     done = []
-    for step in range(width):
-        line = work[step : step + 1, :]
-        scale = lax.rsqrt(work[step : step + 1, step : step + 1])
-        line = line * scale
-        done.append(line)
-        if step + 1 < width:
-            work = work - (work[:, step : step + 1] * scale) * line
+    for base in range(0, width, PANEL):
+        lines = [work[base + i : base + i + 1, :] for i in range(PANEL)]
+        sides = [jnp.broadcast_to(work[:, base + i : base + i + 1], work.shape) for i in range(PANEL)]
+        pivots = {
+            (i, k): jnp.broadcast_to(lines[i][:, base + k : base + k + 1], lines[i].shape)
+            for i in range(PANEL)
+            for k in range(i, PANEL)
+        }
+        change = None
+        for i in range(PANEL):
+            scale = lax.rsqrt(pivots[i, i])
+            line = lines[i] * scale
+            side = sides[i] * scale
+            done.append(line)
+            beta = {k: pivots[i, k] * scale for k in range(i + 1, PANEL)}
+            for k in range(i + 1, PANEL):
+                lines[k] = lines[k] - beta[k] * line
+                sides[k] = sides[k] - beta[k] * side
+                for m in range(k, PANEL):
+                    pivots[k, m] = pivots[k, m] - beta[k] * beta[m]
+            change = side * line if change is None else change + side * line
+        work = work - change
     factor = jnp.concatenate(done, axis=0)
     r_ref[...] = jnp.where(row <= col, factor[:, :width], 0.0)
     inverse = factor[:, width:].T

time: 66.1 us -> 58.4 us (0.88)
  Pallas kernels: 61.1 us -> 53.5 us
    pallas_call x1, Pallas kernels: 12 us -> 7.74 us  [per_device(): pl.pallas_call(feature_kernel, out_shape=(jax.ShapeDtypeStruct((channels...]
    pallas_call x1, Pallas kernels: 6.51 us -> 3.27 us  [per_device(): pl.pallas_call(functools.partial(finish_kernel, root), out_shape=(jax.Sha...]
where the time goes in v4:
time: 58.4 us; the launch traced here: 58.2 us
  Pallas kernels  53.5 us (92%)
  local copies, waits for them, and re-layouts  3.93 us (7%)
  between operations  0.76 us (1%)
    pallas_call x1, Pallas kernels, per_device(): pl.pallas_call(apply_kernel, out_shape=(jax.ShapeDtypeStruct((rows, 2 * w...  42.5 us
    pallas_call x1, Pallas kernels, per_device(): pl.pallas_call(feature_kernel, out_shape=(jax.ShapeDtypeStruct((channels...  7.74 us
    pallas_call x1, Pallas kernels, per_device(): pl.pallas_call(functools.partial(finish_kernel, root), out_shape=(jax.Sha...  3.27 us
    unnamed x21, local copies, waits for them, and re-layouts  3.08 us

profile of v4, /device:TPU:0, one launch (start us, length us, event | category | flops | bytes accessed | tf_op | source)
XLA Modules:
  0.0 58.2 jit_solution(12740785207184253371)
XLA Ops:
  0.6 0.0 copy-start.6
  0.6 1.0 %copy.20.probes_ref.own_ref = bf16[512,64]{1,0:T(8,128)(2,1)S(1)} copy(bf16[512,64]{0,1:T(8,128)(2,1)} %param.17) | data formatting | bytes 131072 | tf_op args[7]
  1.6 0.0 copy-done.6
  1.6 0.0 copy-start.8
  1.7 0.0 copy-start.2
  1.7 0.1 copy.18.tokens_ref
  1.8 0.0 copy-start
  1.8 0.5 copy-done.8
  2.3 0.1 copy.19.inv_len_ref
  2.5 0.0 copy-start.3
  2.5 0.0 copy-start.4
  2.5 0.0 copy-done.2
  2.5 0.2 copy-done
  2.7 0.5 copy-done.3
  3.2 0.0 copy-done.4
  3.2 0.0 copy-start.7
  3.2 7.7 %shard_map.121 = (bf16[336,256]{1,0:T(8,128)(2,1)S(1)}, bf16[256,256]{1,0:T(8,128)(2,1)S(1)}) custom-call(s32[512,69]{1,0:T(8,128)S(1)} %copy.18.tokens_ref, s32[1,512]{1,0:T(1,128)S(1)} %bitcast.3, bf16[64,256]{1,0:T(8,128)(2,1)S(1)} %copy-done.2, bf16[7,32,256]{2,1,0:T(8,128)(2,1)S(1)} %copy-done, f32[1,256]{1,0:T(1,128)S(1)} %bitcast.4, ...), custom_call_target="tpu_custom_call" | custom-call | tf_op jit(solution)/shard_map/pallas_call | solution.py:485
  10.9 0.0 copy-done.7
  10.9 0.0 copy-start.1
  11.0 0.0 copy-start.5
  11.0 0.1 copy.22.prev_ref
  11.1 0.6 %copy-done.1 = f32[64,64]{1,0:T(8,128)S(1)} copy-done((f32[64,64]{1,0:T(8,128)S(1)}, f32[64,64]{1,0:T(8,128)}, u32[]{:S(2)}) %copy-start.1) | copy-done | bytes 16408
  11.7 0.0 copy-done.5
  11.7 42.5 %shard_map.122 = (f32[256,128]{1,0:T(8,128)S(1)}, f32[128,128]{1,0:T(8,128)S(1)}) custom-call(f32[2]{0:T(128)S(1)} %copy-done.5, bf16[256,256]{1,0:T(8,128)(2,1)S(1)} %get-tuple-element.7.rows_ref, bf16[336,256]{1,0:T(8,128)(2,1)S(1)} %get-tuple-element.8.cols_ref, bf16[512,64]{1,0:T(8,128)(2,1)S(1)} %copy.20.probes_ref.own_ref, ...), custom_call_target="tpu_custom_call" | custom-call | tf_op jit(solution)/shard_map/pallas_call | solution.py:508
  54.2 3.3 %shard_map.123 = (f32[64,64]{1,0:T(8,128)}, f32[64,64]{1,0:T(8,128)}, f32[256,64]{1,0:T(8,128)S(1)}) custom-call(f32[256,128]{1,0:T(8,128)S(1)} %get-tuple-element.9.x_ref, f32[128,128]{1,0:T(8,128)S(1)} %get-tuple-element.10.sums_ref), custom_call_target="tpu_custom_call" | custom-call | tf_op jit(solution)/shard_map/pallas_call | solution.py:548
  57.5 0.7 %copy.23 = f32[256,64]{0,1:T(8,128)} copy(f32[256,64]{1,0:T(8,128)S(1)} %get-tuple-element.16) | data formatting | bytes 131072 | tf_op jit(solution)/shard_map/pallas_call | solution.py:548
Async XLA Ops:
  0.6 1.0 %copy-start.6 = (s32[512,69]{0,1:T(8,128)S(1)}, s32[512,69]{0,1:T(8,128)}, u32[]{:S(2)}) copy-start(s32[512,69]{0,1:T(8,128)} %param.10) | copy-start | bytes 423940
  1.6 0.7 %copy-start.8 = (f32[256]{0:T(256)S(1)}, f32[256]{0:T(256)}, u32[]{:S(2)}) copy-start(f32[256]{0:T(256)} %param.15) | copy-start | bytes 3076
  1.7 0.8 %copy-start.2 = (bf16[64,256]{1,0:T(8,128)(2,1)S(1)}, bf16[64,256]{1,0:T(8,128)(2,1)}, u32[]{:S(2)}) copy-start(bf16[64,256]{1,0:T(8,128)(2,1)} %embed_ref.1) | copy-start | bytes 98308
  1.8 0.9 %copy-start = (bf16[7,32,256]{2,1,0:T(8,128)(2,1)S(1)}, bf16[7,32,256]{2,1,0:T(8,128)(2,1)}, u32[]{:S(2)}) copy-start(bf16[7,32,256]{2,1,0:T(8,128)(2,1)} %conv_w_ref.1) | copy-start | bytes 344068
  2.5 0.7 %copy-start.3 = (s32[512]{0:T(512)S(1)}, s32[512]{0:T(512)}, u32[]{:S(2)}) copy-start(s32[512]{0:T(512)} %param.11) | copy-start | bytes 6148
  2.5 0.7 %copy-start.4 = (f32[256]{0:T(256)S(1)}, f32[256]{0:T(256)}, u32[]{:S(2)}) copy-start(f32[256]{0:T(256)} %param.14) | copy-start | bytes 3076
  3.2 7.8 %copy-start.7 = (bf16[256,64]{0,1:T(8,128)(2,1)S(1)}, bf16[256,64]{0,1:T(8,128)(2,1)}, u32[]{:S(2)}) copy-start(bf16[256,64]{0,1:T(8,128)(2,1)} %param.18) | copy-start | bytes 98308
  10.9 0.8 %copy-start.1 = (f32[64,64]{1,0:T(8,128)S(1)}, f32[64,64]{1,0:T(8,128)}, u32[]{:S(2)}) copy-start(f32[64,64]{1,0:T(8,128)} %coupling_ref.1) | copy-start | bytes 49156
  11.0 0.8 %copy-start.5 = (f32[2]{0:T(128)S(1)}, f32[2]{0:T(128)}, u32[]{:S(2)}) copy-start(f32[2]{0:T(128)} %hyper_ref.1) | copy-start | bytes 28

commit v5 on v4

--- a/solution.py
+++ b/solution.py
@@ -147,8 +147,7 @@
     gathered,
     row_send,
     row_recv,
-    up_send,
-    down_send,
+    col_send,
     col_recv,
     side_send,
     side_recv,
@@ -229,13 +228,8 @@
         pl.semaphore_signal(barrier, inc=1, device_id=line_id(peer), device_id_type=pl.DeviceIdType.MESH)
     pl.semaphore_wait(barrier, plane - 1 + line - 1)
 
-    def up_copy(slot, src=None):
-        src = col_blocks.at[slot, core] if src is None else src
-        return copy(src, col_blocks.at[slot, core], up_send.at[slot], col_recv.at[slot], line_id(mine + 1))
-
-    def down_copy(slot, src=None):
-        src = col_blocks.at[slot, core] if src is None else src
-        return copy(src, col_blocks.at[slot, core], down_send.at[slot], col_recv.at[slot], line_id(mine - 1))
+    def col_copy(order, slot, peer):
+        return copy(cols_ref, col_blocks.at[slot, core], col_send.at[order], col_recv.at[slot], line_id(peer))
 
     def side_copy(slot, lane, src=None):
         src = col_blocks.at[slot, lane] if src is None else src
@@ -244,43 +238,15 @@
     def row_copy(step, slot, peer):
         return copy(rows_ref, row_blocks.at[slot], row_send.at[step], row_recv.at[slot], mate_id(peer))
 
-    @pl.when(mine < line - 1)
-    def _():
-        up_copy(mine, cols_ref).start()
-
-    @pl.when(mine > 0)
-    def _():
-        down_copy(mine, cols_ref).start()
-
+    col_copy(1, mine, line_peers[1]).start()
     each_mate(lambda step, peer: row_copy(step, my_mate, peer).start())
+    col_copy(2, mine, line_peers[2]).start()
+    col_copy(3, mine, line_peers[3]).start()
     side_copy(mine, core, cols_ref).start()
     row_blocks[my_mate] = rows_ref[...]
     col_blocks[mine, core] = cols_ref[...]
     amplitude = hyper_ref[0]
 
-    def pass_on(distance):
-        @pl.when(mine >= distance)
-        def _():
-            slot = mine - distance
-            up_copy(slot).wait_recv()
-
-            @pl.when(mine < line - 1)
-            def _():
-                up_copy(slot).start()
-
-            side_copy(slot, core).start()
-
-        @pl.when(mine + distance < line)
-        def _():
-            slot = mine + distance
-            down_copy(slot).wait_recv()
-
-            @pl.when(mine > 0)
-            def _():
-                down_copy(slot).start()
-
-            side_copy(slot, core).start()
-
     def partial_copy(step, slot, peer):
         return copy(
             partial_out.at[step], partial_in.at[slot], partial_send.at[step], partial_recv.at[slot], mate_id(peer)
@@ -290,6 +256,9 @@
         return jnp.concatenate([value[: rows // 2, :], value[rows // 2 :, :]], axis=1)
 
     def column_pass(source, order):
+        if order:
+            col_copy(order, source, source).wait_recv()
+            side_copy(source, core).start()
         side_copy(source, other).wait_recv()
         parts = []
         for lane in range(2):
@@ -338,16 +307,8 @@
 
         lax.fori_loop(0, mates // group, pair_step, 0)
 
-    second = jnp.where(mine == 0, 1, mine - 1)
-    third = jnp.where(mine < 2, 2, jnp.where(mine == 2, 3, 1))
-    fourth = jnp.where(mine < 2, 3, 0)
-    column_pass(mine, 0)
-    pass_on(1)
-    column_pass(second, 1)
-    pass_on(2)
-    column_pass(third, 2)
-    pass_on(3)
-    column_pass(fourth, 3)
+    for order in range(line):
+        column_pass(line_peers[order], order)
 
     own = own_ref[pl.ds(pl.multiple_of(rep * rows, rows), rows), :].astype(F32)
     root = 1.0 / math.sqrt(rows * plane * line)
@@ -406,16 +367,9 @@
         sums_ref[spot * piece : (spot + 1) * piece, :] = gathered[spot]
     for order in range(1, line):
         line_copy(order, mine, line_peers[order]).wait_send()
+        col_copy(order, mine, line_peers[order]).wait_send()
     for slot in range(line):
         side_copy(slot, core).wait_send()
-
-        @pl.when((mine >= slot) & (mine < line - 1))
-        def _(slot=slot):
-            up_copy(slot).wait_send()
-
-        @pl.when((mine <= slot) & (mine > 0))
-        def _(slot=slot):
-            down_copy(slot).wait_send()
 
     def drain_mate(step, peer):
         row_copy(step, my_mate, peer).wait_send()
@@ -530,7 +484,6 @@
             dma((line,)),
             dma((line,)),
             dma((line,)),
-            dma((line,)),
             dma((mates,)),
             dma((mates,)),
             dma((plane,)),

time: 58.4 us -> 56.6 us (0.969)
  Pallas kernels: 53.5 us -> 51.7 us
    pallas_call x1, Pallas kernels: 42.5 us -> 40.7 us  [per_device(): pl.pallas_call(apply_kernel, out_shape=(jax.ShapeDtypeStruct((rows, 2 * w...]
where the time goes in v5:
time: 56.6 us; the launch traced here: 56.4 us
  Pallas kernels  51.7 us (91%)
  local copies, waits for them, and re-layouts  3.93 us (7%)
  between operations  0.76 us (1%)
    pallas_call x1, Pallas kernels, per_device(): pl.pallas_call(apply_kernel, out_shape=(jax.ShapeDtypeStruct((rows, 2 * w...  40.7 us
    pallas_call x1, Pallas kernels, per_device(): pl.pallas_call(feature_kernel, out_shape=(jax.ShapeDtypeStruct((channels...  7.74 us
    pallas_call x1, Pallas kernels, per_device(): pl.pallas_call(functools.partial(finish_kernel, root), out_shape=(jax.Sha...  3.27 us
    unnamed x21, local copies, waits for them, and re-layouts  3.08 us

profile of v5, /device:TPU:0, one launch (start us, length us, event | category | flops | bytes accessed | tf_op | source)
XLA Modules:
  0.0 56.4 jit_solution(14818463750211494271)
XLA Ops:
  0.6 0.0 copy-start.6
  0.6 1.0 %copy.20.probes_ref.own_ref = bf16[512,64]{1,0:T(8,128)(2,1)S(1)} copy(bf16[512,64]{0,1:T(8,128)(2,1)} %param.17) | data formatting | bytes 131072 | tf_op args[7]
  1.6 0.0 copy-done.6
  1.6 0.0 copy-start.8
  1.7 0.0 copy-start.2
  1.7 0.1 copy.18.tokens_ref
  1.8 0.0 copy-start
  1.8 0.5 copy-done.8
  2.3 0.1 copy.19.inv_len_ref
  2.5 0.0 copy-start.3
  2.5 0.0 copy-start.4
  2.5 0.0 copy-done.2
  2.5 0.2 copy-done
  2.7 0.5 copy-done.3
  3.2 0.0 copy-done.4
  3.2 0.0 copy-start.7
  3.2 7.7 %shard_map.121 = (bf16[336,256]{1,0:T(8,128)(2,1)S(1)}, bf16[256,256]{1,0:T(8,128)(2,1)S(1)}) custom-call(s32[512,69]{1,0:T(8,128)S(1)} %copy.18.tokens_ref, s32[1,512]{1,0:T(1,128)S(1)} %bitcast.3, bf16[64,256]{1,0:T(8,128)(2,1)S(1)} %copy-done.2, bf16[7,32,256]{2,1,0:T(8,128)(2,1)S(1)} %copy-done, f32[1,256]{1,0:T(1,128)S(1)} %bitcast.4, ...), custom_call_target="tpu_custom_call" | custom-call | tf_op jit(solution)/shard_map/pallas_call | solution.py:439
  10.9 0.0 copy-done.7
  10.9 0.0 copy-start.1
  11.0 0.0 copy-start.5
  11.0 0.1 copy.22.prev_ref
  11.1 0.6 %copy-done.1 = f32[64,64]{1,0:T(8,128)S(1)} copy-done((f32[64,64]{1,0:T(8,128)S(1)}, f32[64,64]{1,0:T(8,128)}, u32[]{:S(2)}) %copy-start.1) | copy-done | bytes 16408
  11.7 0.0 copy-done.5
  11.7 40.7 %shard_map.122 = (f32[256,128]{1,0:T(8,128)S(1)}, f32[128,128]{1,0:T(8,128)S(1)}) custom-call(f32[2]{0:T(128)S(1)} %copy-done.5, bf16[256,256]{1,0:T(8,128)(2,1)S(1)} %get-tuple-element.7.rows_ref, bf16[336,256]{1,0:T(8,128)(2,1)S(1)} %get-tuple-element.8.cols_ref, bf16[512,64]{1,0:T(8,128)(2,1)S(1)} %copy.20.probes_ref.own_ref, ...), custom_call_target="tpu_custom_call" | custom-call | tf_op jit(solution)/shard_map/pallas_call | solution.py:462
  52.4 3.3 %shard_map.123 = (f32[64,64]{1,0:T(8,128)}, f32[64,64]{1,0:T(8,128)}, f32[256,64]{1,0:T(8,128)S(1)}) custom-call(f32[256,128]{1,0:T(8,128)S(1)} %get-tuple-element.9.x_ref, f32[128,128]{1,0:T(8,128)S(1)} %get-tuple-element.10.sums_ref), custom_call_target="tpu_custom_call" | custom-call | tf_op jit(solution)/shard_map/pallas_call | solution.py:501
  55.6 0.7 %copy.23 = f32[256,64]{0,1:T(8,128)} copy(f32[256,64]{1,0:T(8,128)S(1)} %get-tuple-element.16) | data formatting | bytes 131072 | tf_op jit(solution)/shard_map/pallas_call | solution.py:501
Async XLA Ops:
  0.6 1.0 %copy-start.6 = (s32[512,69]{0,1:T(8,128)S(1)}, s32[512,69]{0,1:T(8,128)}, u32[]{:S(2)}) copy-start(s32[512,69]{0,1:T(8,128)} %param.10) | copy-start | bytes 423940
  1.6 0.7 %copy-start.8 = (f32[256]{0:T(256)S(1)}, f32[256]{0:T(256)}, u32[]{:S(2)}) copy-start(f32[256]{0:T(256)} %param.15) | copy-start | bytes 3076
  1.7 0.8 %copy-start.2 = (bf16[64,256]{1,0:T(8,128)(2,1)S(1)}, bf16[64,256]{1,0:T(8,128)(2,1)}, u32[]{:S(2)}) copy-start(bf16[64,256]{1,0:T(8,128)(2,1)} %embed_ref.1) | copy-start | bytes 98308
  1.8 0.9 %copy-start = (bf16[7,32,256]{2,1,0:T(8,128)(2,1)S(1)}, bf16[7,32,256]{2,1,0:T(8,128)(2,1)}, u32[]{:S(2)}) copy-start(bf16[7,32,256]{2,1,0:T(8,128)(2,1)} %conv_w_ref.1) | copy-start | bytes 344068
  2.5 0.7 %copy-start.3 = (s32[512]{0:T(512)S(1)}, s32[512]{0:T(512)}, u32[]{:S(2)}) copy-start(s32[512]{0:T(512)} %param.11) | copy-start | bytes 6148
  2.5 0.7 %copy-start.4 = (f32[256]{0:T(256)S(1)}, f32[256]{0:T(256)}, u32[]{:S(2)}) copy-start(f32[256]{0:T(256)} %param.14) | copy-start | bytes 3076
  3.2 7.8 %copy-start.7 = (bf16[256,64]{0,1:T(8,128)(2,1)S(1)}, bf16[256,64]{0,1:T(8,128)(2,1)}, u32[]{:S(2)}) copy-start(bf16[256,64]{0,1:T(8,128)(2,1)} %param.18) | copy-start | bytes 98308
  10.9 0.8 %copy-start.1 = (f32[64,64]{1,0:T(8,128)S(1)}, f32[64,64]{1,0:T(8,128)}, u32[]{:S(2)}) copy-start(f32[64,64]{1,0:T(8,128)} %coupling_ref.1) | copy-start | bytes 49156
  11.0 0.8 %copy-start.5 = (f32[2]{0:T(128)S(1)}, f32[2]{0:T(128)}, u32[]{:S(2)}) copy-start(f32[2]{0:T(128)} %hyper_ref.1) | copy-start | bytes 28

commit v6 on v5

--- a/solution.py
+++ b/solution.py
@@ -85,7 +85,6 @@
     conv_w_ref,
     conv_b_ref,
     inv_len_ref,
-    probes_ref,
     cols_ref,
     rows_ref,
     padded,
@@ -122,19 +121,35 @@
     order = lax.broadcasted_iota(jnp.int32, (EXTRA, rows), 0)
     tail = jnp.where(order == 0, high, jnp.where(order == 1, middle, jnp.where(order == 2, low, 0.0)))
     cols_ref[channels : channels + EXTRA, :] = tail.astype(BF16)
-    cols_ref[channels + EXTRA :, :] = probes_ref[pl.ds(first, rows), :].astype(F32).T.astype(BF16)
     rows_ref[...] = wide.T.astype(BF16)
 
 
 def apply_kernel(
     hyper_ref,
-    rows_ref,
-    cols_ref,
+    tokens_ref,
+    lengths_ref,
+    embed_ref,
+    conv_w_ref,
+    conv_b_ref,
+    inv_len_ref,
     own_ref,
     prev_ref,
     coupling_ref,
     x_ref,
     sums_ref,
+    cols_ref,
+    rows_ref,
+    padded,
+    onehot,
+    table,
+    table_hi,
+    table_lo,
+    pooled,
+    probe_blocks,
+    probe_send,
+    probe_recv,
+    share_send,
+    share_recv,
     row_blocks,
     col_blocks,
     row_halves,
@@ -226,7 +241,40 @@
     each_plane_peer(greet)
     for peer in line_peers[1:]:
         pl.semaphore_signal(barrier, inc=1, device_id=line_id(peer), device_id_type=pl.DeviceIdType.MESH)
+    own = own_ref[pl.ds(pl.multiple_of(rep * rows, rows), rows), :].astype(F32)
+    probe_blocks[core, mine] = own.T.astype(BF16)
     pl.semaphore_wait(barrier, plane - 1 + line - 1)
+
+    def probe_copy(order, slot, peer):
+        return copy(
+            probe_blocks.at[core, mine],
+            probe_blocks.at[core, slot],
+            probe_send.at[order],
+            probe_recv.at[slot],
+            line_id(peer),
+        )
+
+    def share_copy(lane):
+        return copy(probe_blocks.at[lane], probe_blocks.at[lane], share_send.at[0], share_recv.at[0], sibling)
+
+    for order in range(1, line):
+        probe_copy(order, mine, line_peers[order]).start()
+    feature_kernel(
+        tokens_ref,
+        lengths_ref,
+        embed_ref,
+        conv_w_ref,
+        conv_b_ref,
+        inv_len_ref,
+        cols_ref,
+        rows_ref,
+        padded,
+        onehot,
+        table,
+        table_hi,
+        table_lo,
+        pooled,
+    )
 
     def col_copy(order, slot, peer):
         return copy(cols_ref, col_blocks.at[slot, core], col_send.at[order], col_recv.at[slot], line_id(peer))
@@ -246,6 +294,20 @@
     row_blocks[my_mate] = rows_ref[...]
     col_blocks[mine, core] = cols_ref[...]
     amplitude = hyper_ref[0]
+    for order in range(1, line):
+        probe_copy(order, line_peers[order], line_peers[order]).wait_recv()
+    share_copy(core).start()
+    root = 1.0 / math.sqrt(rows * plane * line)
+    coupled = lax.dot_general(
+        prev_ref[...].astype(F32),
+        coupling_ref[...],
+        (((1,), (1,)), ((), ())),
+        precision=HIGH,
+        preferred_element_type=F32,
+    )
+    x_ref[:, :width] = own * root
+    x_ref[:, width:] = (hyper_ref[1] * own - coupled) * root
+    share_copy(other).wait_recv()
 
     def partial_copy(step, slot, peer):
         return copy(
@@ -264,7 +326,7 @@
         for lane in range(2):
             cols = col_blocks.at[source, lane]
             col_half = jnp.sum(cols[channels : channels + EXTRA, :].astype(F32), axis=0, keepdims=True)
-            block_probes = cols[channels + EXTRA :, :].astype(F32).T.astype(BF16)
+            block_probes = probe_blocks[lane, source].astype(F32).T.astype(BF16)
             parts.append((cols, col_half, block_probes))
         last = order == line - 1
 
@@ -310,16 +372,6 @@
     for order in range(line):
         column_pass(line_peers[order], order)
 
-    own = own_ref[pl.ds(pl.multiple_of(rep * rows, rows), rows), :].astype(F32)
-    root = 1.0 / math.sqrt(rows * plane * line)
-    coupled = lax.dot_general(
-        prev_ref[...].astype(F32),
-        coupling_ref[...],
-        (((1,), (1,)), ((), ())),
-        precision=HIGH,
-        preferred_element_type=F32,
-    )
-
     def add_partial(step, total):
         spot = mate_peer(step)
         partial_copy(step, spot, spot).wait_recv()
@@ -327,8 +379,7 @@
 
     total = lax.fori_loop(1, mates, add_partial, partial_out[mates])
     applied = jnp.concatenate([total[:, :width], total[:, width:]], axis=0)
-    x_ref[:, :width] = own * root
-    x_ref[:, width:] = (applied + hyper_ref[1] * own - coupled) * root
+    x_ref[:, width:] += applied * root
     both = x_ref[...]
     gram = jnp.dot(both.T, both, precision=HIGH, preferred_element_type=F32)
     piece = gram_out.shape[1]
@@ -368,6 +419,8 @@
     for order in range(1, line):
         line_copy(order, mine, line_peers[order]).wait_send()
         col_copy(order, mine, line_peers[order]).wait_send()
+        probe_copy(order, mine, line_peers[order]).wait_send()
+    share_copy(core).wait_send()
     for slot in range(line):
         side_copy(slot, core).wait_send()
 
@@ -436,24 +489,6 @@
     taps = conv_w.shape[0]
     seq = tokens.shape[1]
     depth = taps * vocab
-    cols, own_rows = pl.pallas_call(
-        feature_kernel,
-        out_shape=(
-            jax.ShapeDtypeStruct((channels + EXTRA + width, rows), BF16),
-            jax.ShapeDtypeStruct((rows, channels), BF16),
-        ),
-        in_specs=[VMEM] * 7,
-        out_specs=(VMEM, VMEM),
-        scratch_shapes=[
-            pltpu.VMEM((rows, 128), jnp.int32),
-            pltpu.VMEM((seq * vocab, rows), BF16),
-            pltpu.VMEM((depth, channels), F32),
-            pltpu.VMEM((channels, depth), BF16),
-            pltpu.VMEM((channels, depth), BF16),
-            pltpu.VMEM((channels, rows), F32),
-        ],
-        compiler_params=PARAMS,
-    )(tokens, lengths.reshape(1, -1), embed, conv_w, conv_b.reshape(1, -1), inv_len.reshape(-1, 1), probes)
     line = LINE
     plane = lax.axis_size("blk") // line * lax.axis_size("rep")
     mates = plane // 2
@@ -465,11 +500,24 @@
             jax.ShapeDtypeStruct((rows, 2 * width), F32),
             jax.ShapeDtypeStruct((2 * width, 2 * width), F32),
         ),
-        in_specs=[SMEM] + [VMEM] * 5,
+        in_specs=[SMEM] + [VMEM] * 9,
         out_specs=(VMEM, VMEM),
         scratch_shapes=[
+            pltpu.VMEM((channels + EXTRA, rows), BF16),
+            pltpu.VMEM((rows, channels), BF16),
+            pltpu.VMEM((rows, 128), jnp.int32),
+            pltpu.VMEM((seq * vocab, rows), BF16),
+            pltpu.VMEM((depth, channels), F32),
+            pltpu.VMEM((channels, depth), BF16),
+            pltpu.VMEM((channels, depth), BF16),
+            pltpu.VMEM((channels, rows), F32),
+            pltpu.VMEM((2, line, width, rows), BF16),
+            dma((line,)),
+            dma((line,)),
+            dma((1,)),
+            dma((1,)),
             pltpu.VMEM((mates, rows, channels), BF16),
-            pltpu.VMEM((line, 2, channels + EXTRA + width, rows), BF16),
+            pltpu.VMEM((line, 2, channels + EXTRA, rows), BF16),
             pltpu.VMEM((mates, rows, 1), F32),
             pltpu.VMEM((mates, rows, width), F32),
             pltpu.VMEM((mates + 1, rows // 2, 2 * width), F32),
@@ -496,7 +544,18 @@
         compiler_params=pltpu.CompilerParams(
             vmem_limit_bytes=48 * 1024 * 1024, collective_id=0, has_side_effects=True
         ),
-    )(hyper, own_rows, cols, probes, prev_probes, coupling)
+    )(
+        hyper,
+        tokens,
+        lengths.reshape(1, -1),
+        embed,
+        conv_w,
+        conv_b.reshape(1, -1),
+        inv_len.reshape(-1, 1),
+        probes,
+        prev_probes,
+        coupling,
+    )
     root = math.sqrt(rows * plane * line)
     return pl.pallas_call(
         functools.partial(finish_kernel, root),

time: 56.6 us -> 55 us (0.972)
  Pallas kernels: 51.7 us -> 50.7 us
    pallas_call x1 -> x0, Pallas kernels: 7.74 us -> none  [per_device(): pl.pallas_call(feature_kernel, out_shape=(jax.ShapeDtypeStruct((channels...]
    pallas_call x1, Pallas kernels: 40.7 us -> 47.4 us  [per_device(): pl.pallas_call(apply_kernel, out_shape=(jax.ShapeDtypeStruct((rows, 2 * w...]
where the time goes in v6:
time: 55 us; the launch traced here: 54.8 us
  Pallas kernels  50.7 us (92%)
  local copies, waits for them, and re-layouts  3.39 us (6%)
  between operations  0.74 us (1%)
    pallas_call x1, Pallas kernels, per_device(): pl.pallas_call(apply_kernel, out_shape=(jax.ShapeDtypeStruct((rows, 2 * w...  47.4 us
    pallas_call x1, Pallas kernels, per_device(): pl.pallas_call(functools.partial(finish_kernel, root), out_shape=(jax.Sha...  3.27 us
    unnamed x21, local copies, waits for them, and re-layouts  2.54 us

profile of v6, /device:TPU:0, one launch (start us, length us, event | category | flops | bytes accessed | tf_op | source)
XLA Modules:
  0.0 54.8 jit_solution(8559096511408661600)
XLA Ops:
  0.6 0.0 copy-start.8
  0.6 0.0 copy-start.7
  0.7 0.9 %copy.20.prev_ref = bf16[256,64]{1,0:T(8,128)(2,1)S(1)} copy(bf16[256,64]{0,1:T(8,128)(2,1)} %param.18) | data formatting | bytes 65536 | tf_op args[8]
  1.6 0.0 copy-done.8
  1.6 0.0 copy-start.6
  1.6 0.1 copy.18.inv_len_ref
  1.7 0.0 copy-done.7
  1.7 0.1 copy.19.own_ref
  1.9 0.6 %copy-done.6 = s32[512,69]{0,1:T(8,128)S(1)} copy-done((s32[512,69]{0,1:T(8,128)S(1)}, s32[512,69]{0,1:T(8,128)}, u32[]{:S(2)}) %copy-start.6) | copy-done | bytes 141336
  2.5 0.0 copy-start
  2.5 0.0 copy-start.1
  2.5 0.0 copy-start.2
  2.5 0.0 copy-start.3
  2.5 0.0 copy-start.4
  2.5 0.0 copy-start.5
  2.5 0.1 copy.17.tokens_ref
  2.6 0.7 %copy-done = bf16[7,32,256]{2,1,0:T(8,128)(2,1)S(1)} copy-done((bf16[7,32,256]{2,1,0:T(8,128)(2,1)S(1)}, bf16[7,32,256]{2,1,0:T(8,128)(2,1)}, u32[]{:S(2)}) %copy-start) | copy-done | bytes 114712
  3.4 0.0 copy-done.1
  3.4 0.0 copy-done.2
  3.4 0.0 copy-done.3
  3.4 0.0 copy-done.4
  3.4 0.0 copy-done.5
  3.4 47.4 %shard_map.121 = (f32[256,128]{1,0:T(8,128)S(1)}, f32[128,128]{1,0:T(8,128)S(1)}) custom-call(f32[2]{0:T(128)S(1)} %copy-done.5, s32[512,69]{1,0:T(8,128)S(1)} %copy.17.tokens_ref, s32[1,512]{1,0:T(1,128)S(1)} %bitcast.3, bf16[64,256]{1,0:T(8,128)(2,1)S(1)} %copy-done.1, bf16[7,32,256]{2,1,0:T(8,128)(2,1)S(1)} %copy-done, f32[1,256]{1,0:T(1,128)S(1)} %bitcast.4, ...), custom_call_target="tpu_custom_call" | custom-call | tf_op jit(solution)/shard_map/pallas_call | solution.py:497
  50.8 3.3 %shard_map.122 = (f32[64,64]{1,0:T(8,128)}, f32[64,64]{1,0:T(8,128)}, f32[256,64]{1,0:T(8,128)S(1)}) custom-call(f32[256,128]{1,0:T(8,128)S(1)} %get-tuple-element.5.x_ref, f32[128,128]{1,0:T(8,128)S(1)} %get-tuple-element.6.sums_ref), custom_call_target="tpu_custom_call" | custom-call | tf_op jit(solution)/shard_map/pallas_call | solution.py:560
  54.1 0.7 %copy.21 = f32[256,64]{0,1:T(8,128)} copy(f32[256,64]{1,0:T(8,128)S(1)} %get-tuple-element.12) | data formatting | bytes 131072 | tf_op jit(solution)/shard_map/pallas_call | solution.py:560
Async XLA Ops:
  0.6 0.9 %copy-start.8 = (f32[256]{0:T(256)S(1)}, f32[256]{0:T(256)}, u32[]{:S(2)}) copy-start(f32[256]{0:T(256)} %param.15) | copy-start | bytes 3076
  0.6 1.1 %copy-start.7 = (bf16[512,64]{0,1:T(8,128)(2,1)S(1)}, bf16[512,64]{0,1:T(8,128)(2,1)}, u32[]{:S(2)}) copy-start(bf16[512,64]{0,1:T(8,128)(2,1)} %param.17) | copy-start | bytes 196612
  1.6 0.9 %copy-start.6 = (s32[512,69]{0,1:T(8,128)S(1)}, s32[512,69]{0,1:T(8,128)}, u32[]{:S(2)}) copy-start(s32[512,69]{0,1:T(8,128)} %param.10) | copy-start | bytes 423940
  2.5 0.9 %copy-start = (bf16[7,32,256]{2,1,0:T(8,128)(2,1)S(1)}, bf16[7,32,256]{2,1,0:T(8,128)(2,1)}, u32[]{:S(2)}) copy-start(bf16[7,32,256]{2,1,0:T(8,128)(2,1)} %conv_w_ref.1) | copy-start | bytes 344068
  2.5 0.9 %copy-start.1 = (bf16[64,256]{1,0:T(8,128)(2,1)S(1)}, bf16[64,256]{1,0:T(8,128)(2,1)}, u32[]{:S(2)}) copy-start(bf16[64,256]{1,0:T(8,128)(2,1)} %embed_ref.1) | copy-start | bytes 98308
  2.5 0.9 %copy-start.2 = (f32[64,64]{1,0:T(8,128)S(1)}, f32[64,64]{1,0:T(8,128)}, u32[]{:S(2)}) copy-start(f32[64,64]{1,0:T(8,128)} %coupling_ref.1) | copy-start | bytes 49156
  2.5 0.9 %copy-start.3 = (s32[512]{0:T(512)S(1)}, s32[512]{0:T(512)}, u32[]{:S(2)}) copy-start(s32[512]{0:T(512)} %param.11) | copy-start | bytes 6148
  2.5 0.9 %copy-start.4 = (f32[256]{0:T(256)S(1)}, f32[256]{0:T(256)}, u32[]{:S(2)}) copy-start(f32[256]{0:T(256)} %param.14) | copy-start | bytes 3076
  2.5 0.9 %copy-start.5 = (f32[2]{0:T(128)S(1)}, f32[2]{0:T(128)}, u32[]{:S(2)}) copy-start(f32[2]{0:T(128)} %hyper_ref.1) | copy-start | bytes 28

commit v7 on v6

--- a/solution.py
+++ b/solution.py
@@ -317,60 +317,55 @@
     def packed(value):
         return jnp.concatenate([value[: rows // 2, :], value[rows // 2 :, :]], axis=1)
 
-    def column_pass(source, order):
+    def column_pass(source, lane, first, last):
+        cols = col_blocks.at[source, lane]
+        col_half = jnp.sum(cols[channels : channels + EXTRA, :].astype(F32), axis=0, keepdims=True)
+        block_probes = probe_blocks[lane, source].astype(F32).T.astype(BF16)
+        group = 1 if first else 2 if last else 4
+
+        def group_step(index, carry):
+            steps = [group * index + part + (1 if last else 0) for part in range(group)]
+            if first:
+                for step in steps:
+                    spot = mate_peer(step)
+
+                    @pl.when(step > 0)
+                    def _():
+                        row_copy(step, spot, spot).wait_recv()
+
+                    wide = row_blocks[spot].astype(F32)
+                    row_halves[spot] = -0.5 * jnp.sum(wide * wide, axis=1, keepdims=True)
+            values = []
+            for step in steps:
+                spot = mate_peer(step)
+                inner = jnp.dot(row_blocks[spot], cols[:channels, :], preferred_element_type=F32)
+                exponent = jnp.minimum(inner + (row_halves[spot] + col_half), 0.0)
+                weights = (amplitude * jnp.exp(exponent)).astype(BF16)
+                value = jnp.dot(weights, block_probes, preferred_element_type=F32)
+                values.append(value if first else value + totals[spot])
+            for step, value in zip(steps, values):
+                spot = mate_peer(step)
+                if not last:
+                    totals[spot] = value
+                    continue
+                partial_out[step] = packed(value)
+
+                @pl.when(step < mates)
+                def _():
+                    partial_copy(step, my_mate, spot).start()
+
+            return carry
+
+        lax.fori_loop(0, mates // group, group_step, 0)
+
+    for order in range(line):
+        source = line_peers[order]
         if order:
             col_copy(order, source, source).wait_recv()
             side_copy(source, core).start()
+        column_pass(source, core, order == 0, False)
         side_copy(source, other).wait_recv()
-        parts = []
-        for lane in range(2):
-            cols = col_blocks.at[source, lane]
-            col_half = jnp.sum(cols[channels : channels + EXTRA, :].astype(F32), axis=0, keepdims=True)
-            block_probes = probe_blocks[lane, source].astype(F32).T.astype(BF16)
-            parts.append((cols, col_half, block_probes))
-        last = order == line - 1
-
-        group = 1 if order == 0 else 2
-
-        def pair_step(pair, carry):
-            steps = [group * pair + part + (1 if last else 0) for part in range(group)]
-            if order == 0:
-                for step in steps:
-                    spot = mate_peer(step)
-
-                    @pl.when(step > 0)
-                    def _():
-                        row_copy(step, spot, spot).wait_recv()
-
-                    wide = row_blocks[spot].astype(F32)
-                    row_halves[spot] = -0.5 * jnp.sum(wide * wide, axis=1, keepdims=True)
-            for step in steps:
-                spot = mate_peer(step)
-                value = None if order == 0 else totals[spot]
-                for cols, col_half, block_probes in parts:
-                    inner = jnp.dot(row_blocks[spot], cols[:channels, :], preferred_element_type=F32)
-                    exponent = jnp.minimum(inner + (row_halves[spot] + col_half), 0.0)
-                    weights = (amplitude * jnp.exp(exponent)).astype(BF16)
-                    term = jnp.dot(weights, block_probes, preferred_element_type=F32)
-                    value = term if value is None else value + term
-                if last:
-                    partial_out[step] = packed(value)
-                else:
-                    totals[spot] = value
-            if last:
-                for step in steps:
-                    spot = mate_peer(step)
-
-                    @pl.when(step < mates)
-                    def _():
-                        partial_copy(step, my_mate, spot).start()
-
-            return carry
-
-        lax.fori_loop(0, mates // group, pair_step, 0)
-
-    for order in range(line):
-        column_pass(line_peers[order], order)
+        column_pass(source, other, False, order == line - 1)
 
     def add_partial(step, total):
         spot = mate_peer(step)

time: 55 us -> 53.4 us (0.971)
  Pallas kernels: 50.7 us -> 49.1 us
    pallas_call x1, Pallas kernels: 47.4 us -> 45.9 us  [per_device(): pl.pallas_call(apply_kernel, out_shape=(jax.ShapeDtypeStruct((rows, 2 * w...]
where the time goes in v7:
time: 53.4 us; the launch traced here: 53.2 us
  Pallas kernels  49.1 us (92%)
  local copies, waits for them, and re-layouts  3.39 us (6%)
  between operations  0.74 us (1%)
    pallas_call x1, Pallas kernels, per_device(): pl.pallas_call(apply_kernel, out_shape=(jax.ShapeDtypeStruct((rows, 2 * w...  45.9 us
    pallas_call x1, Pallas kernels, per_device(): pl.pallas_call(functools.partial(finish_kernel, root), out_shape=(jax.Sha...  3.27 us
    unnamed x21, local copies, waits for them, and re-layouts  2.54 us

profile of v7, /device:TPU:0, one launch (start us, length us, event | category | flops | bytes accessed | tf_op | source)
XLA Modules:
  0.0 53.2 jit_solution(14124908632975675224)
XLA Ops:
  0.6 0.0 copy-start.8
  0.6 0.0 copy-start.7
  0.7 0.9 %copy.20.prev_ref = bf16[256,64]{1,0:T(8,128)(2,1)S(1)} copy(bf16[256,64]{0,1:T(8,128)(2,1)} %param.18) | data formatting | bytes 65536 | tf_op args[8]
  1.6 0.0 copy-done.8
  1.6 0.0 copy-start.6
  1.6 0.1 copy.18.inv_len_ref
  1.7 0.0 copy-done.7
  1.7 0.1 copy.19.own_ref
  1.9 0.6 %copy-done.6 = s32[512,69]{0,1:T(8,128)S(1)} copy-done((s32[512,69]{0,1:T(8,128)S(1)}, s32[512,69]{0,1:T(8,128)}, u32[]{:S(2)}) %copy-start.6) | copy-done | bytes 141336
  2.5 0.0 copy-start
  2.5 0.0 copy-start.1
  2.5 0.0 copy-start.2
  2.5 0.0 copy-start.3
  2.5 0.0 copy-start.4
  2.5 0.0 copy-start.5
  2.5 0.1 copy.17.tokens_ref
  2.6 0.7 %copy-done = bf16[7,32,256]{2,1,0:T(8,128)(2,1)S(1)} copy-done((bf16[7,32,256]{2,1,0:T(8,128)(2,1)S(1)}, bf16[7,32,256]{2,1,0:T(8,128)(2,1)}, u32[]{:S(2)}) %copy-start) | copy-done | bytes 114712
  3.4 0.0 copy-done.1
  3.4 0.0 copy-done.2
  3.4 0.0 copy-done.3
  3.4 0.0 copy-done.4
  3.4 0.0 copy-done.5
  3.4 45.9 %shard_map.121 = (f32[256,128]{1,0:T(8,128)S(1)}, f32[128,128]{1,0:T(8,128)S(1)}) custom-call(f32[2]{0:T(128)S(1)} %copy-done.5, s32[512,69]{1,0:T(8,128)S(1)} %copy.17.tokens_ref, s32[1,512]{1,0:T(1,128)S(1)} %bitcast.3, bf16[64,256]{1,0:T(8,128)(2,1)S(1)} %copy-done.1, bf16[7,32,256]{2,1,0:T(8,128)(2,1)S(1)} %copy-done, f32[1,256]{1,0:T(1,128)S(1)} %bitcast.4, ...), custom_call_target="tpu_custom_call" | custom-call | tf_op jit(solution)/shard_map/pallas_call | solution.py:492
  49.3 3.3 %shard_map.122 = (f32[64,64]{1,0:T(8,128)}, f32[64,64]{1,0:T(8,128)}, f32[256,64]{1,0:T(8,128)S(1)}) custom-call(f32[256,128]{1,0:T(8,128)S(1)} %get-tuple-element.5.x_ref, f32[128,128]{1,0:T(8,128)S(1)} %get-tuple-element.6.sums_ref), custom_call_target="tpu_custom_call" | custom-call | tf_op jit(solution)/shard_map/pallas_call | solution.py:555
  52.5 0.7 %copy.21 = f32[256,64]{0,1:T(8,128)} copy(f32[256,64]{1,0:T(8,128)S(1)} %get-tuple-element.12) | data formatting | bytes 131072 | tf_op jit(solution)/shard_map/pallas_call | solution.py:555
Async XLA Ops:
  0.6 0.9 %copy-start.8 = (f32[256]{0:T(256)S(1)}, f32[256]{0:T(256)}, u32[]{:S(2)}) copy-start(f32[256]{0:T(256)} %param.15) | copy-start | bytes 3076
  0.6 1.1 %copy-start.7 = (bf16[512,64]{0,1:T(8,128)(2,1)S(1)}, bf16[512,64]{0,1:T(8,128)(2,1)}, u32[]{:S(2)}) copy-start(bf16[512,64]{0,1:T(8,128)(2,1)} %param.17) | copy-start | bytes 196612
  1.6 0.9 %copy-start.6 = (s32[512,69]{0,1:T(8,128)S(1)}, s32[512,69]{0,1:T(8,128)}, u32[]{:S(2)}) copy-start(s32[512,69]{0,1:T(8,128)} %param.10) | copy-start | bytes 423940
  2.5 0.9 %copy-start = (bf16[7,32,256]{2,1,0:T(8,128)(2,1)S(1)}, bf16[7,32,256]{2,1,0:T(8,128)(2,1)}, u32[]{:S(2)}) copy-start(bf16[7,32,256]{2,1,0:T(8,128)(2,1)} %conv_w_ref.1) | copy-start | bytes 344068
  2.5 0.9 %copy-start.1 = (bf16[64,256]{1,0:T(8,128)(2,1)S(1)}, bf16[64,256]{1,0:T(8,128)(2,1)}, u32[]{:S(2)}) copy-start(bf16[64,256]{1,0:T(8,128)(2,1)} %embed_ref.1) | copy-start | bytes 98308
  2.5 0.9 %copy-start.2 = (f32[64,64]{1,0:T(8,128)S(1)}, f32[64,64]{1,0:T(8,128)}, u32[]{:S(2)}) copy-start(f32[64,64]{1,0:T(8,128)} %coupling_ref.1) | copy-start | bytes 49156
  2.5 0.9 %copy-start.3 = (s32[512]{0:T(512)S(1)}, s32[512]{0:T(512)}, u32[]{:S(2)}) copy-start(s32[512]{0:T(512)} %param.11) | copy-start | bytes 6148
  2.5 0.9 %copy-start.4 = (f32[256]{0:T(256)S(1)}, f32[256]{0:T(256)}, u32[]{:S(2)}) copy-start(f32[256]{0:T(256)} %param.14) | copy-start | bytes 3076
  2.5 0.9 %copy-start.5 = (f32[2]{0:T(128)S(1)}, f32[2]{0:T(128)}, u32[]{:S(2)}) copy-start(f32[2]{0:T(128)} %hyper_ref.1) | copy-start | bytes 28

commit v8 on v7

--- a/solution.py
+++ b/solution.py
@@ -12,8 +12,8 @@
 BF16 = jnp.bfloat16
 EXTRA = 16
 LINE = 4
-GROUP = 4
-PANEL = 4
+GROUP = 8
+PANEL = 8
 HIGH = lax.Precision.HIGHEST
 
 

time: 53.4 us -> 52 us (0.974)
  Pallas kernels: 49.1 us -> 47.7 us
    pallas_call x1, Pallas kernels: 45.9 us -> 44.8 us  [per_device(): pl.pallas_call(apply_kernel, out_shape=(jax.ShapeDtypeStruct((rows, 2 * w...]
where the time goes in v8:
time: 52 us; the launch traced here: 51.8 us
  Pallas kernels  47.7 us (92%)
  local copies, waits for them, and re-layouts  3.39 us (7%)
  between operations  0.74 us (1%)
    pallas_call x1, Pallas kernels, per_device(): pl.pallas_call(apply_kernel, out_shape=(jax.ShapeDtypeStruct((rows, 2 * w...  44.8 us
    pallas_call x1, Pallas kernels, per_device(): pl.pallas_call(functools.partial(finish_kernel, root), out_shape=(jax.Sha...  2.82 us
    unnamed x21, local copies, waits for them, and re-layouts  2.54 us

profile of v8, /device:TPU:0, one launch (start us, length us, event | category | flops | bytes accessed | tf_op | source)
XLA Modules:
  0.0 51.8 jit_solution(6328088085113928879)
XLA Ops:
  0.6 0.0 copy-start.8
  0.6 0.0 copy-start.7
  0.7 0.9 %copy.20.prev_ref = bf16[256,64]{1,0:T(8,128)(2,1)S(1)} copy(bf16[256,64]{0,1:T(8,128)(2,1)} %param.18) | data formatting | bytes 65536 | tf_op args[8]
  1.6 0.0 copy-done.8
  1.6 0.0 copy-start.6
  1.6 0.1 copy.18.inv_len_ref
  1.7 0.0 copy-done.7
  1.7 0.1 copy.19.own_ref
  1.9 0.6 %copy-done.6 = s32[512,69]{0,1:T(8,128)S(1)} copy-done((s32[512,69]{0,1:T(8,128)S(1)}, s32[512,69]{0,1:T(8,128)}, u32[]{:S(2)}) %copy-start.6) | copy-done | bytes 141336
  2.5 0.0 copy-start
  2.5 0.0 copy-start.1
  2.5 0.0 copy-start.2
  2.5 0.0 copy-start.3
  2.5 0.0 copy-start.4
  2.5 0.0 copy-start.5
  2.5 0.1 copy.17.tokens_ref
  2.6 0.7 %copy-done = bf16[7,32,256]{2,1,0:T(8,128)(2,1)S(1)} copy-done((bf16[7,32,256]{2,1,0:T(8,128)(2,1)S(1)}, bf16[7,32,256]{2,1,0:T(8,128)(2,1)}, u32[]{:S(2)}) %copy-start) | copy-done | bytes 114712
  3.4 0.0 copy-done.1
  3.4 0.0 copy-done.2
  3.4 0.0 copy-done.3
  3.4 0.0 copy-done.4
  3.4 0.0 copy-done.5
  3.4 44.8 %shard_map.121 = (f32[256,128]{1,0:T(8,128)S(1)}, f32[128,128]{1,0:T(8,128)S(1)}) custom-call(f32[2]{0:T(128)S(1)} %copy-done.5, s32[512,69]{1,0:T(8,128)S(1)} %copy.17.tokens_ref, s32[1,512]{1,0:T(1,128)S(1)} %bitcast.3, bf16[64,256]{1,0:T(8,128)(2,1)S(1)} %copy-done.1, bf16[7,32,256]{2,1,0:T(8,128)(2,1)S(1)} %copy-done, f32[1,256]{1,0:T(1,128)S(1)} %bitcast.4, ...), custom_call_target="tpu_custom_call" | custom-call | tf_op jit(solution)/shard_map/pallas_call | solution.py:492
  48.3 2.8 %shard_map.122 = (f32[64,64]{1,0:T(8,128)}, f32[64,64]{1,0:T(8,128)}, f32[256,64]{1,0:T(8,128)S(1)}) custom-call(f32[256,128]{1,0:T(8,128)S(1)} %get-tuple-element.5.x_ref, f32[128,128]{1,0:T(8,128)S(1)} %get-tuple-element.6.sums_ref), custom_call_target="tpu_custom_call" | custom-call | tf_op jit(solution)/shard_map/pallas_call | solution.py:555
  51.1 0.7 %copy.21 = f32[256,64]{0,1:T(8,128)} copy(f32[256,64]{1,0:T(8,128)S(1)} %get-tuple-element.12) | data formatting | bytes 131072 | tf_op jit(solution)/shard_map/pallas_call | solution.py:555
Async XLA Ops:
  0.6 0.9 %copy-start.8 = (f32[256]{0:T(256)S(1)}, f32[256]{0:T(256)}, u32[]{:S(2)}) copy-start(f32[256]{0:T(256)} %param.15) | copy-start | bytes 3076
  0.6 1.1 %copy-start.7 = (bf16[512,64]{0,1:T(8,128)(2,1)S(1)}, bf16[512,64]{0,1:T(8,128)(2,1)}, u32[]{:S(2)}) copy-start(bf16[512,64]{0,1:T(8,128)(2,1)} %param.17) | copy-start | bytes 196612
  1.6 0.9 %copy-start.6 = (s32[512,69]{0,1:T(8,128)S(1)}, s32[512,69]{0,1:T(8,128)}, u32[]{:S(2)}) copy-start(s32[512,69]{0,1:T(8,128)} %param.10) | copy-start | bytes 423940
  2.5 0.9 %copy-start = (bf16[7,32,256]{2,1,0:T(8,128)(2,1)S(1)}, bf16[7,32,256]{2,1,0:T(8,128)(2,1)}, u32[]{:S(2)}) copy-start(bf16[7,32,256]{2,1,0:T(8,128)(2,1)} %conv_w_ref.1) | copy-start | bytes 344068
  2.5 0.9 %copy-start.1 = (bf16[64,256]{1,0:T(8,128)(2,1)S(1)}, bf16[64,256]{1,0:T(8,128)(2,1)}, u32[]{:S(2)}) copy-start(bf16[64,256]{1,0:T(8,128)(2,1)} %embed_ref.1) | copy-start | bytes 98308
  2.5 0.9 %copy-start.2 = (f32[64,64]{1,0:T(8,128)S(1)}, f32[64,64]{1,0:T(8,128)}, u32[]{:S(2)}) copy-start(f32[64,64]{1,0:T(8,128)} %coupling_ref.1) | copy-start | bytes 49156
  2.5 0.9 %copy-start.3 = (s32[512]{0:T(512)S(1)}, s32[512]{0:T(512)}, u32[]{:S(2)}) copy-start(s32[512]{0:T(512)} %param.11) | copy-start | bytes 6148
  2.5 0.9 %copy-start.4 = (f32[256]{0:T(256)S(1)}, f32[256]{0:T(256)}, u32[]{:S(2)}) copy-start(f32[256]{0:T(256)} %param.14) | copy-start | bytes 3076
  2.5 0.9 %copy-start.5 = (f32[2]{0:T(128)S(1)}, f32[2]{0:T(128)}, u32[]{:S(2)}) copy-start(f32[2]{0:T(128)} %hyper_ref.1) | copy-start | bytes 28
